TPU v7x, 256 devices: a whole 4x4x8 slice. The times are simulated.
256 devices in a mesh: sec: 4 (over x_lo, core), col: 64 (over y, x_hi, z).
Axes of the slice: x: 4 (x_hi: 2, x_lo: 2; x = x_hi * 2 + x_lo), y: 4, z: 8, core: 2. Of those that a mesh axis runs over, the one named last changes fastest.
Arguments:
- column_state: float32 [16384, 128], P('col'), may hold values from -6 to 6
- mixing_rate: float32 [128], replicated, may hold values from 0.05 to 0.2
- neighbours: int32 [4096, 4], P('col'), may hold values from 0 to 4095, as said below
- assignment: int32 [16384, 1], P('col'), may hold values from 0 to 191; in each aligned block of 256 rows (0 to 255, 256 to 511, ...) at most 2 rows name the same one
- substeps: int32 [16384], P('col'), may hold values from 1 to 4
- cloud_state: bfloat16 [4, 2, 58, 32, 8192], P('sec', None, None, None, 'col'), may hold values from -6 to 6
- level_map: float32 [58, 64], replicated, may hold values from -0.75 to 0.75
- saturation: float32 [58], replicated, may hold values from -0.5 to 0.5
Outputs:
- new_columns: float32 [16384, 128], P('col')
- new_cloud_state: bfloat16 [4, 2, 58, 32, 8192], P('sec', None, None, None, 'col')
Inputs may be any that keep to these rules, and one draw needn't show every extreme that they name: `neighbours`: each neighbour lies within 64 elements of its own element in the order of elements that wraps around, and some lie exactly 64 away. `assignment`: in each aligned block of 256 columns no cloud device is named by more than 2 columns, and in some block one is named by exactly 2.
All inputs are finite; a program needn't handle non-finite values.
Results may differ from a plain program's by a relative error of at most 0.001.
Values sent between devices are 32-bit elements; how exact they have to be, the bound alone decides.
A program may use at most 64 MiB of HBM per device.

v0:
```python
import jax
import jax.numpy as jnp
from jax import lax
from jax.sharding import PartitionSpec as P

MAX_SUB = 4


RELAX = 0.25
HORIZ = 0.12
VERTIC = 0.1
LATENT = 2.5
VMIX = 0.2
HIGH = lax.Precision.HIGHEST


def extended_2(cells, sides, width):
    for axis, dim in sides:
        count = lax.axis_size(axis)
        head = lax.slice_in_dim(cells, 0, width, axis=dim)
        tail = lax.slice_in_dim(cells, cells.shape[dim] - width, cells.shape[dim], axis=dim)
        cells = jnp.concatenate(
            [
                lax.ppermute(tail, axis, [(i, (i + 1) % count) for i in range(count)]),
                cells,
                lax.ppermute(head, axis, [((i + 1) % count, i) for i in range(count)]),
            ],
            axis=dim,
        )
    return cells


def vertical_term(values, levels):
    shaped = values.reshape(values.shape[0], -1, levels)
    upper = jnp.concatenate([shaped[:, :, 1:], shaped[:, :, -1:]], axis=2)
    lower = jnp.concatenate([shaped[:, :, :1], shaped[:, :, :-1]], axis=2)
    return (upper + lower - 2.0 * shaped).reshape(values.shape)


def advance(columns, mixing_rate, element_means, near_ids, own_means, levels):
    spread = jnp.sum(element_means[near_ids], axis=1) - 4.0 * own_means
    return (
        columns
        + mixing_rate[None, :] * jnp.repeat(spread, 4, axis=0)
        + VMIX * vertical_term(columns, levels)
    )


def slot_ranks(targets, destinations):
    onehot = (targets[:, None] == jnp.arange(destinations, dtype=jnp.int32)[None, :]).astype(
        jnp.int32
    )
    running = jnp.cumsum(onehot, axis=0) - 1
    return jnp.sum(running * onehot, axis=1)


def cloud_substep(fields, target, saturation):
    mean_now = jnp.mean(fields, axis=2)
    fields = fields + RELAX * (target - mean_now)[:, :, None, :]
    across = jnp.roll(fields, 1, axis=2) + jnp.roll(fields, -1, axis=2) - 2.0 * fields
    upper = jnp.concatenate([fields[:, 1:], fields[:, -1:]], axis=1)
    lower = jnp.concatenate([fields[:, :1], fields[:, :-1]], axis=1)
    fields = fields + HORIZ * across + VERTIC * (upper + lower - 2.0 * fields)
    condensed = 0.5 * jnp.maximum(fields[1] - saturation[:, None, None], 0.0)
    return jnp.stack([fields[0] + LATENT * condensed, fields[1] - condensed])


def run_cloud(block, columns, counts, level_map, saturation, levels):
    shaped = columns.reshape(columns.shape[0], -1, levels)
    target = jnp.einsum("zl,sfl->fzs", level_map, shaped, precision=HIGH)
    start = block.astype(jnp.float32)
    fields = start
    for substep_index in range(MAX_SUB):
        stepped = cloud_substep(fields, target, saturation)
        fields = jnp.where((counts > substep_index)[None, None, None, :], stepped, fields)
    change = jnp.mean(fields, axis=2) - jnp.mean(start, axis=2)
    tendency = jnp.einsum("zl,fzs->sfl", level_map, change, precision=HIGH).reshape(
        columns.shape[0], -1
    )
    return (fields.astype(jnp.bfloat16), tendency)


def body(
    column_state, mixing_rate, neighbours, assignment, substeps, cloud_state, level_map, saturation
):
    col_count = lax.axis_size("col")
    section = lax.axis_index("sec")
    position = lax.axis_index("col")
    host_rows = column_state.shape[0]
    width = column_state.shape[1]
    levels = level_map.shape[1]
    elements = host_rows // 4
    own_means = jnp.mean(column_state.reshape(-1, 4, width), axis=1)
    extended = extended_2(column_state, (("col", 0),), host_rows)
    ext_means = jnp.mean(extended.reshape(-1, 4, width), axis=1)
    near_ids = jnp.mod(neighbours - (position - 1) * elements, elements * col_count)
    advanced = advance(column_state, mixing_rate, ext_means, near_ids, own_means, levels)
    per_device = cloud_state.shape[-1]
    capacity = per_device // col_count
    targets = assignment[:, 0]
    ranks = slot_ranks(targets, (lax.axis_size("sec") - 1) * col_count)
    mine = targets // col_count + 1 == section
    slot_index = jnp.where(mine, targets % col_count * capacity + ranks, per_device)
    outgoing = jnp.zeros((per_device, width), jnp.float32).at[slot_index].set(advanced, mode="drop")
    out_counts = jnp.zeros((per_device,), jnp.int32).at[slot_index].set(substeps, mode="drop")
    incoming, in_counts = (
        lax.all_to_all(outgoing, "col", split_axis=0, concat_axis=0, tiled=True),
        lax.all_to_all(out_counts, "col", split_axis=0, concat_axis=0, tiled=True),
    )
    new_block, tendency = run_cloud(
        cloud_state[0], incoming, in_counts, level_map, saturation, levels
    )
    returned = lax.all_to_all(tendency, "col", split_axis=0, concat_axis=0, tiled=True)
    own_tendency = jnp.where(mine[:, None], returned[jnp.minimum(slot_index, per_device - 1)], 0.0)
    contribution = jnp.where(section == 0, advanced, own_tendency)
    is_water = (jnp.arange(width) // levels == 1)[None, :]
    summed = lax.psum(contribution, "sec")
    new_columns = jnp.where(is_water, jnp.maximum(summed, 0.0), summed)
    return (new_columns, new_block[None])


def solution(mesh):
    in_specs = (
        P("col", None),
        P(),
        P("col", None),
        P("col", None),
        P("col"),
        P("sec", None, None, None, "col"),
        P(),
        P(),
    )
    out_specs = (P("col", None), P("sec", None, None, None, "col"))
    return jax.shard_map(body, mesh=mesh, in_specs=in_specs, out_specs=out_specs, check_vma=False)
```

profile of v0, /device:TPU:1, one launch (start us, length us, event | category | flops | bytes accessed | tf_op | source)
XLA Modules:
  0.0 143.2 jit_solution(10716387471098084238)
XLA Ops:
  7.2 11.4 %collective-permute-start.1 = (f32[256,128]{1,0:T(8,128)}, f32[256,128]{1,0:T(8,128)S(1)}, u32[]{:S(2)}, u32[]{:S(2)}) collective-permute-start(f32[256,128]{1,0:T(8,128)} %param.8), channel_id=1, source_target_pairs={{1,0},{2,1},{3,2},{4,3},{5,4},{6,5},{7,6},{8,7},{9,8},{10,9},{11,1... | collective-permute-start | bytes 393224 | tf_op jit(solution)/shard_map/ppermute | solution.py:26
  18.6 0.7 compare_reduce_fusion.4
  19.3 0.8 copy.24
  20.6 0.7 fusion.34
  21.4 0.7 compare_select_fusion
  22.1 1.6 %scatter_custom_fusion = s32[128]{0:T(128)S(1)} fusion(s32[256]{0:T(256)S(1)} %bitcast.89, s32[256]{0:T(256)} %param.12, s32[]{:T(128)} %constant.101.clone.1), kind=kCustom, calls=%fused_computation.124 | custom fusion | bytes 1024 | tf_op jit(solution)/shard_map/scatter | solution.py:105
  23.6 0.8 all_to_all.20
  24.4 9.5 %all-to-all-start = ((s32[64,2,1]{1,2,0:T(1,128)}), s32[64,2,1]{1,2,0:T(1,128)S(1)}, u32[]{:S(2)}, u32[]{:S(2)}) async-start(s32[64,2,1]{1,2,0:T(1,128)} %bitcast.12), calls=%async_computation | async-start | bytes 65536 | tf_op jit(solution)/shard_map/all_to_all | solution.py:108
  33.9 1.0 copy.22
  35.7 0.7 gather_fusion
  36.6 1.7 %scatter_custom_fusion.1 = f32[128,128]{1,0:T(8,128)} fusion(s32[256]{0:T(256)S(1)} %bitcast.90, f32[256,128]{1,0:T(8,128)S(1)} %multiply_add_fusion, f32[]{:T(128)} %constant.106.clone.1), kind=kCustom, calls=%fused_computation.97 | custom fusion | bytes 65540 | tf_op jit(solution)/shard_map/scatter | solution.py:104
  38.4 6.2 %all-to-all-done = s32[64,2,1]{1,2,0:T(1,128)S(1)} async-done(((s32[64,2,1]{1,2,0:T(1,128)}), s32[64,2,1]{1,2,0:T(1,128)S(1)}, u32[]{:S(2)}, u32[]{:S(2)}) %all-to-all-start) | async-done | bytes 544 | tf_op jit(solution)/shard_map/all_to_all | solution.py:108
  44.6 6.2 %all-to-all-start.1 = ((f32[64,2,128]{2,1,0:T(2,128)}), f32[64,2,128]{2,1,0:T(2,128)S(1)}, u32[]{:S(2)}, u32[]{:S(2)}) async-start(f32[64,2,128]{2,1,0:T(2,128)} %bitcast.14), calls=%async_computation.1 | async-start | bytes 131072 | tf_op jit(solution)/shard_map/all_to_all | solution.py:107
  52.1 9.5 %all-to-all-done.1 = f32[64,2,128]{2,1,0:T(2,128)S(1)} async-done(((f32[64,2,128]{2,1,0:T(2,128)}), f32[64,2,128]{2,1,0:T(2,128)S(1)}, u32[]{:S(2)}, u32[]{:S(2)}) %all-to-all-start.1) | async-done | bytes 65568 | tf_op jit(solution)/shard_map/all_to_all | solution.py:107
  63.4 1.1 fusion.9
  66.3 0.6 fusion.67
  67.0 1.9 %fusion.15 = f32[2,58,32,128]{3,2,1,0:T(8,128)S(1)} fusion(f32[2,58,31,128]{3,2,1,0:T(8,128)S(1)} %get-tuple-element.43, f32[2,58,1,128]{3,2,1,0:T(1,128)S(1)} %get-tuple-element.45, f32[2,58,1,128]{3,2,1,0:T(1,128)S(1)} %get-tuple-element.44, f32[2,58,31,128]{3,2,1,0:T(8,128)S(1)} %get-tuple-element.42, f32[2,1,32,128]{3,2,1,0:T(8,128)S(1)} %get-tuple-element.39, ...), kind=kLoop, calls=%fused_computation.25 | loop fusion | flops 8077312 | bytes 12413056 | tf_op jit(solution)/shard_map/add | solution.py:63
  69.2 0.7 fusion.56
  71.3 0.6 fusion.63
  71.9 1.3 fusion.21
  73.5 0.6 fusion.55
  75.6 0.6 fusion.59
  76.2 1.3 fusion.27
  77.7 0.7 fusion.30
  79.4 0.8 all_to_all.24
  80.2 4.6 %all-to-all-start.2 = ((f32[64,2,128]{2,1,0:T(2,128)}), f32[64,2,128]{2,1,0:T(2,128)S(1)}, u32[]{:S(2)}, u32[]{:S(2)}) async-start(f32[64,2,128]{2,1,0:T(2,128)} %all_to_all.24), calls=%async_computation.2 | async-start | bytes 131072 | tf_op jit(solution)/shard_map/all_to_all | solution.py:113
  84.9 10.9 %all-to-all-done.2 = f32[64,2,128]{2,1,0:T(2,128)S(1)} async-done(((f32[64,2,128]{2,1,0:T(2,128)}), f32[64,2,128]{2,1,0:T(2,128)S(1)}, u32[]{:S(2)}, u32[]{:S(2)}) %all-to-all-start.2) | async-done | bytes 65568 | tf_op jit(solution)/shard_map/all_to_all | solution.py:113
  95.8 0.7 gather_fusion.1
  96.5 0.8 select_select_fusion
  97.3 4.6 %fusion.5 = bf16[1,2,58,32,128]{4,3,2,1,0:T(8,128)(2,1)} fusion(bf16[1,2,58,32,128]{4,3,2,1,0:T(8,128)(2,1)S(1)} %copy-done.1, f32[1,1,58,32,128]{4,3,2,1,0:T(8,128)} %bitcast.76, f32[1,1,58,32,128]{4,3,2,1,0:T(8,128)} %bitcast.75, f32[1,1,58,32,128]{4,3,2,1,0:T(8,128)} %bitcast.74, f32[1,1,58,32,128]{4,3,2,1,0:T(8,128)} %bitcast.73, ...), kind=kLoop, calls=%fused_computation.12 | loop fusion | flops 9977856 | bytes 9503232 | tf_op jit(solution)/shard_map/convert_element_type | solution.py:80
  101.9 32.9 %all-reduce.2.cloned.1.call-done = f32[256,128]{1,0:T(8,128)} async-done(((f32[256,128]{1,0:T(8,128)}), f32[256,128]{1,0:T(8,128)}) %all-reduce.2.cloned.1.call-update) | async-done | bytes 131088 | tf_op jit(solution)/shard_map/psum | solution.py:117
  134.8 1.6 %maximum_select_fusion.3 = f32[256,128]{1,0:T(8,128)} fusion(f32[256,128]{1,0:T(8,128)} %all-reduce.2.cloned.1.call-done, pred[128]{0:T(512)(128)(4,1)S(1)} %fusion.50), kind=kLoop, calls=%fused_computation.74 | loop fusion | flops 65536 | bytes 262272 | tf_op jit(solution)/shard_map/jit(_where)/select_n | solution.py:118
  (89 shorter events, 10.9 us)
Async XLA Ops:
  7.2 54.6 %copy-start = (f32[58,64]{1,0:T(8,128)S(1)}, f32[58,64]{1,0:T(8,128)}, u32[]{:S(2)}) copy-start(f32[58,64]{1,0:T(8,128)} %param.14) | copy-start | bytes 44548
  7.2 28.1 %copy-start.8 = (f32[256,128]{1,0:T(8,128)S(1)}, f32[256,128]{1,0:T(8,128)}, u32[]{:S(2)}) copy-start(f32[256,128]{1,0:T(8,128)} %param.8) | copy-start | bytes 393220
  7.2 27.7 %copy-start.10 = (s32[64,4]{0,1:T(4,128)S(1)}, s32[64,4]{0,1:T(4,128)}, u32[]{:S(2)}) copy-start(s32[64,4]{0,1:T(4,128)} %param.10) | copy-start | bytes 3076
  7.2 28.2 %collective-permute-start.1 = (f32[256,128]{1,0:T(8,128)}, f32[256,128]{1,0:T(8,128)S(1)}, u32[]{:S(2)}, u32[]{:S(2)}) collective-permute-start(f32[256,128]{1,0:T(8,128)} %param.8), channel_id=1, source_target_pairs={{1,0},{2,1},{3,2},{4,3},{5,4},{6,5},{7,6},{8,7},{9,8},{10,9},{11,1... | collective-permute-start | bytes 393224 | tf_op jit(solution)/shard_map/ppermute | solution.py:26
  18.6 16.8 %collective-permute-start = (f32[256,128]{1,0:T(8,128)}, f32[256,128]{1,0:T(8,128)S(1)}, u32[]{:S(2)}, u32[]{:S(2)}) collective-permute-start(f32[256,128]{1,0:T(8,128)} %param.8), channel_id=1, source_target_pairs={{0,1},{1,2},{2,3},{3,4},{4,5},{5,6},{6,7},{7,8},{8,9},{9,10},{10,1... | collective-permute-start | bytes 393224 | tf_op jit(solution)/shard_map/ppermute | solution.py:24
  24.4 20.2 %all-to-all-start = ((s32[64,2,1]{1,2,0:T(1,128)}), s32[64,2,1]{1,2,0:T(1,128)S(1)}, u32[]{:S(2)}, u32[]{:S(2)}) async-start(s32[64,2,1]{1,2,0:T(1,128)} %bitcast.12), calls=%async_computation | async-start | bytes 65536 | tf_op jit(solution)/shard_map/all_to_all | solution.py:108
  35.0 1.6 %copy-start.11 = (f32[128]{0:T(128)S(1)}, f32[128]{0:T(128)}, u32[]{:S(2)}) copy-start(f32[128]{0:T(128)} %param.9) | copy-start | bytes 1540
  35.4 15.4 %copy-start.1 = (bf16[1,2,58,32,128]{4,3,2,1,0:T(8,128)(2,1)S(1)}, bf16[1,2,58,32,128]{4,3,2,1,0:T(8,128)(2,1)}, u32[]{:S(2)}) copy-start(bf16[1,2,58,32,128]{4,3,2,1,0:T(8,128)(2,1)} %param.13) | copy-start | bytes 2850820
  44.6 17.0 %all-to-all-start.1 = ((f32[64,2,128]{2,1,0:T(2,128)}), f32[64,2,128]{2,1,0:T(2,128)S(1)}, u32[]{:S(2)}, u32[]{:S(2)}) async-start(f32[64,2,128]{2,1,0:T(2,128)} %bitcast.14), calls=%async_computation.1 | async-start | bytes 131072 | tf_op jit(solution)/shard_map/all_to_all | solution.py:107
  63.4 1.1 copy-start.9
  69.1 1.0 copy-start.2
  69.1 1.3 copy-start.3
  73.5 1.1 copy-start.4
  73.5 1.2 copy-start.5
  77.7 1.0 copy-start.6
  77.7 1.3 copy-start.7
  80.2 15.6 %all-to-all-start.2 = ((f32[64,2,128]{2,1,0:T(2,128)}), f32[64,2,128]{2,1,0:T(2,128)S(1)}, u32[]{:S(2)}, u32[]{:S(2)}) async-start(f32[64,2,128]{2,1,0:T(2,128)} %all_to_all.24), calls=%async_computation.2 | async-start | bytes 131072 | tf_op jit(solution)/shard_map/all_to_all | solution.py:113
  84.8 50.0 %all-reduce.2.cloned.1.call-start = ((), (), s32[]{:S(2)}) async-start(), calls=%async_computation.3 | async-start | bytes 262144 | tf_op jit(solution)/shard_map/psum | solution.py:117
Sparse Core Ops, SparseCore 0:
  97.4 37.3 all-reduce.1
where the time goes:
time: 144 us; the launch traced here: 143 us
  waiting for transfers between devices  59.5 us (41%)
  starting transfers between devices  31.7 us (22%)
  other arithmetic  21 us (15%)
  local copies, waits for them, and re-layouts  15.8 us (11%)
  between operations  14.7 us (10%)
    psum x1, waiting for transfers between devices, body(): summed = lax.psum(contribution, 'sec')  32.9 us
    ppermute x1, starting transfers between devices, extended_2(): lax.ppermute(head, axis, [((i + 1) % count, i) for i in range(count)])  11.4 us
    all_to_all x1, waiting for transfers between devices, body(): lax.all_to_all(tendency, 'col', split_axis=0, concat_axis=0, tiled=True)  10.9 us
    all_to_all x1, waiting for transfers between devices, body(): lax.all_to_all(outgoing, 'col', split_axis=0, concat_axis=0, tiled=True)  9.5 us
    all_to_all x1, starting transfers between devices, body(): lax.all_to_all(out_counts, 'col', split_axis=0, concat_axis=0, tiled=True)  9.47 us
    all_to_all x1, waiting for transfers between devices, body(): lax.all_to_all(out_counts, 'col', split_axis=0, concat_axis=0, tiled=True)  6.19 us
    all_to_all x1, starting transfers between devices, body(): lax.all_to_all(outgoing, 'col', split_axis=0, concat_axis=0, tiled=True)  6.18 us
    add x4, other arithmetic, cloud_substep(): fields = fields + HORIZ * across + VERTIC * (upper + lower - 2.0 * fields)  5.53 us
  transfers between devices with their start and end apart: 6, of which 4 were waited for; matrix products, arithmetic and copies ran while one was open for 11% of the time, Pallas kernels for 0%

commit v1 on v0

v1 whole, which is shorter than its diff:
```python
import functools

import jax
import jax.numpy as jnp
from jax import lax
from jax.experimental import pallas as pl
from jax.experimental.pallas import tpu as pltpu
from jax.sharding import PartitionSpec as P

MAX_SUB = 4
RELAX = 0.25
HORIZ = 0.12
VERTIC = 0.1
LATENT = 2.5
VMIX = 0.2
MESH = pl.DeviceIdType.MESH
F32 = jnp.float32
BF16 = jnp.bfloat16
I32 = jnp.int32
NN = (((1,), (0,)), ((), ()))
NT = (((1,), (1,)), ((), ()))


def iota(shape, dim):
    return lax.broadcasted_iota(I32, shape, dim)


def halves(x):
    hi = x.astype(BF16)
    return hi, (x - hi.astype(F32)).astype(BF16)


def dot(a, b, dims=NN):
    return lax.dot_general(a, b, dims, preferred_element_type=F32)


def pick(exact, x, dims=NN):
    hi, lo = halves(x)
    return dot(exact, hi, dims) + dot(exact, lo, dims)


def dot3(x, y, dims=NN):
    xh, xl = halves(x)
    yh, yl = halves(y)
    return dot(xh, yh, dims) + (dot(xh, yl, dims) + dot(xl, yh, dims))


def kernel(
    sizes,
    cs_ref,
    rate_ref,
    nbr_ref,
    asg_ref,
    cnt_ref,
    cloud_ref,
    map_ref,
    sat_ref,
    out_ref,
    new_cloud_ref,
    block,
    plain,
    state,
    parts,
    shift_rows,
    square,
    means,
    halo,
    disp_send,
    disp_recv,
    tend_send,
    tends,
    adv_ref,
    local_sem,
    halo_send_sem,
    halo_recv_sem,
    disp_send_sem,
    disp_recv_sem,
    tend_send_sem,
    tend_recv_sem,
    group_send_sem,
    group_recv_sem,
):
    n_sec, n_col = sizes
    sec, col = lax.axis_index("sec"), lax.axis_index("col")
    rows, width = cs_ref.shape
    elements = rows // 4
    total = elements * n_col
    cap, slots = disp_send.shape[1], n_col * disp_send.shape[1]
    levels_c, levels_h = map_ref.shape
    left, right = lax.rem(col + n_col - 1, n_col), lax.rem(col + 1, n_col)
    is_cloud = sec > 0

    barrier = pltpu.get_barrier_semaphore()

    for step in range(1, n_sec):
        pl.semaphore_signal(
            barrier, inc=1, device_id=(lax.rem(sec + step, n_sec), col), device_id_type=MESH
        )

    @pl.when(is_cloud)
    def _():
        def greet(step, carry):
            pl.semaphore_signal(
                barrier, inc=1, device_id=(sec, lax.rem(col + step, n_col)), device_id_type=MESH
            )
            return carry

        lax.fori_loop(1, n_col, greet, 0)

    @pl.when(jnp.logical_not(is_cloud))
    def _():
        for other in (left, right):
            pl.semaphore_signal(barrier, inc=1, device_id=(sec, other), device_id_type=MESH)

    fetch = pltpu.make_async_copy(cloud_ref.at[0], block, local_sem.at[0])
    fetch.start()

    own = (
        cs_ref[pl.ds(0, elements, stride=4), :]
        + cs_ref[pl.ds(1, elements, stride=4), :]
        + cs_ref[pl.ds(2, elements, stride=4), :]
        + cs_ref[pl.ds(3, elements, stride=4), :]
    ) * 0.25
    means[...] = own

    @pl.when(is_cloud)
    def _():
        pl.semaphore_wait(barrier, n_sec - 1 + n_col - 1)

    @pl.when(jnp.logical_not(is_cloud))
    def _():
        pl.semaphore_wait(barrier, n_sec - 1 + 2)

    to_right = pltpu.make_async_remote_copy(
        src_ref=means, dst_ref=halo.at[0], send_sem=halo_send_sem.at[0], recv_sem=halo_recv_sem.at[0],
        device_id=(sec, right), device_id_type=MESH,
    )
    to_left = pltpu.make_async_remote_copy(
        src_ref=means, dst_ref=halo.at[1], send_sem=halo_send_sem.at[1], recv_sem=halo_recv_sem.at[1],
        device_id=(sec, left), device_id_type=MESH,
    )
    to_right.start()
    to_left.start()

    asg = asg_ref[...]
    asg_column = jnp.transpose(jnp.broadcast_to(asg.astype(F32), (128, rows)))[:, 0:1]
    same = (asg_column == asg.astype(F32)) & (iota((rows, rows), 0) < iota((rows, rows), 1))
    rank = jnp.max(jnp.where(same, 1.0, 0.0), axis=0, keepdims=True)
    slot = (asg * cap).astype(F32) + rank
    slot_column = jnp.transpose(jnp.broadcast_to(slot, (128, rows)))[:, 0:1]

    place = iota((3 * elements, elements), 0)
    place = jnp.where(
        place < elements, place, jnp.where(place < 2 * elements, place + elements, place - elements)
    )
    near = jnp.where(place == elements + iota((3 * elements, elements), 1), -4.0, 0.0)
    relative = jnp.bitwise_and(nbr_ref[...] - (col - 1) * elements, total - 1)
    for k in range(4):
        near = near + jnp.where(relative[k : k + 1, :] == place, 1.0, 0.0)
    near_t = near.astype(BF16)
    near_e = jnp.transpose(
        jnp.concatenate([near, jnp.zeros((3 * elements, 128 - elements), F32)], axis=1)
    )[:elements].astype(BF16)

    cs = cs_ref[...]
    lane = jnp.bitwise_and(iota((rows, width), 1), levels_h - 1)
    upper = jnp.where(lane == levels_h - 1, cs, pltpu.roll(cs, width - 1, axis=1))
    lower = jnp.where(lane == 0, cs, pltpu.roll(cs, 1, axis=1))
    base = cs + VMIX * (upper + lower - 2.0 * cs)
    rate = rate_ref[...]

    square[...] = jnp.zeros_like(square)
    square[0:levels_c, 0:levels_h] = map_ref[...]
    square[levels_h : levels_h + levels_c, levels_h : 2 * levels_h] = map_ref[...]

    @pl.when(is_cloud)
    def _():
        chosen = iota((slots, rows), 0) + (sec - 1) * slots == slot.astype(I32)
        chosen32 = jnp.where(chosen, 1.0, 0.0)
        chosen16 = chosen32.astype(BF16)
        counts = jnp.sum(chosen32 * cnt_ref[...].astype(F32), axis=1, keepdims=True)
        repeat = jnp.where(
            iota((elements, rows), 0) == lax.shift_right_logical(iota((elements, rows), 1), 2), 1.0, 0.0
        ).astype(BF16)
        by_element = dot(chosen16, repeat, NT).astype(BF16)
        reach = dot(by_element, near_t, NT).astype(BF16)
        known = pick(chosen16, base) + rate * pick(reach[:, 2 * elements :], own)
        reach = reach[:, : 2 * elements]

        to_right.wait_recv()
        to_left.wait_recv()
        outside = halo[...].reshape(2 * elements, width)
        sent = known + rate * pick(reach, outside)
        target = dot3(sent, square[...], NT)
        target = jnp.where(iota((slots, width), 1) == levels_c, counts, target)
        disp_send[...] = target.reshape(n_col, cap, width)

        def send(step, carry):
            other = lax.rem(col + step, n_col)
            pltpu.make_async_remote_copy(
                src_ref=disp_send.at[other], dst_ref=disp_recv.at[col],
                send_sem=disp_send_sem, recv_sem=disp_recv_sem,
                device_id=(sec, other), device_id_type=MESH,
            ).start()
            return carry

        lax.fori_loop(1, n_col, send, 0)
        pltpu.make_async_copy(disp_send.at[col], disp_recv.at[col], disp_recv_sem).start()

        fetch.wait()
        parts[...] = jnp.zeros_like(parts)

        for f in range(2):

            def widen(z, carry, f=f):
                x = block[f, z].astype(F32)
                plain[f, z] = x
                parts[f, z] = (x[0:8] + x[8:16]) + (x[16:24] + x[24:32])
                return carry

            lax.fori_loop(0, levels_c, widen, 0, unroll=2)

        def strided(f, z):
            return tuple(plain[f, z, pl.ds(k, 8, stride=4), :] for k in range(4))

        def packed(f, z):
            return tuple(state[f, z, pl.ds(8 * k, 8), :] for k in range(4))

        def stencil(here, below, above):
            west = (pltpu.roll(here[3], 1, axis=0),) + here[:3]
            east = here[1:] + (pltpu.roll(here[0], 7, axis=0),)
            return tuple(
                (1.0 - 2.0 * HORIZ - 2.0 * VERTIC) * here[k]
                + HORIZ * (east[k] + west[k])
                + VERTIC * (above[k] + below[k])
                for k in range(4)
            )

        for f in range(2):

            def first(z, carry, f=f):
                below, here = carry
                above = strided(f, jnp.minimum(z + 1, levels_c - 1))
                new = stencil(here, below, above)
                for k in range(4):
                    state[f, z, pl.ds(8 * k, 8), :] = new[k]
                return here, above

            edge = strided(f, 0)
            lax.fori_loop(0, levels_c, first, (edge, edge), unroll=2)

        columns_inv = 1.0 / plain.shape[2]
        start = [jnp.sum(parts[f], axis=1) * columns_inv for f in range(2)]
        level = iota((levels_h, slots), 0)

        def vertical(x):
            up = jnp.where(level == levels_c - 1, x, pltpu.roll(x, levels_h - 1, axis=0))
            low = jnp.where(level == 0, x, pltpu.roll(x, 1, axis=0))
            return VERTIC * (up + low - 2.0 * x)

        pltpu.make_async_copy(disp_recv, disp_recv, disp_recv_sem).wait()
        arrived = jnp.transpose(disp_recv[...].reshape(slots, width))
        counts = arrived[levels_c : levels_c + 1, :]
        goal = [arrived[f * levels_h : (f + 1) * levels_h] for f in range(2)]
        mean = list(start)

        def condense(a, f_shift, z, keep, old):
            half = 0.5 * sat_ref[z]
            new0, new1, drop = [], [], []
            for k in range(4):
                water = a[1][k] + f_shift[1]
                c = jnp.maximum(0.5 * water - half, 0.0)
                new1.append(jnp.where(keep, water - c, old[1][k]))
                new0.append(jnp.where(keep, (a[0][k] + f_shift[0]) + LATENT * c, old[0][k]))
                drop.append(c)
            parts[0, z] = (drop[0] + drop[1]) + (drop[2] + drop[3])
            return new0, new1

        for n in range(MAX_SUB):
            keep = counts > float(n)
            keep_tile = jnp.broadcast_to(counts, (8, slots)) > float(n)
            moved = []
            for f in range(2):
                d = RELAX * (goal[f] - mean[f])
                d = d + vertical(d)
                shift_rows[f] = d
                moved.append(mean[f] + vertical(mean[f]) + d)

            def shifts(z):
                return [
                    jnp.broadcast_to(shift_rows[f, pl.ds(z, 1), :], (8, slots)) for f in range(2)
                ]

            if n == 0:

                def finish(z, carry):
                    new = condense(
                        (packed(0, z), packed(1, z)), shifts(z), z, keep_tile,
                        (strided(0, z), strided(1, z)),
                    )
                    for f in range(2):
                        for k in range(4):
                            state[f, z, pl.ds(8 * k, 8), :] = new[f][k]
                    return carry

                lax.fori_loop(0, levels_c, finish, 0, unroll=2)
            else:

                def sweep(z, carry, last=n == MAX_SUB - 1):
                    below, here = carry
                    following = jnp.minimum(z + 1, levels_c - 1)
                    above = (packed(0, following), packed(1, following))
                    a = [stencil(here[f], below[f], above[f]) for f in range(2)]
                    new = condense(a, shifts(z), z, keep_tile, here)
                    for f in range(2):
                        for k in range(4):
                            if last:
                                plain[f, z, pl.ds(k, 8, stride=4), :] = new[f][k]
                            else:
                                state[f, z, pl.ds(8 * k, 8), :] = new[f][k]
                    return here, above

                edge = (packed(0, 0), packed(1, 0))
                lax.fori_loop(0, levels_c, sweep, (edge, edge), unroll=2)

            dried = jnp.sum(parts[0], axis=1) * columns_inv
            mean[0] = jnp.where(keep, moved[0] + LATENT * dried, mean[0])
            mean[1] = jnp.where(keep, moved[1] - dried, mean[1])

        change = jnp.concatenate(
            [jnp.where(level < levels_c, mean[f] - start[f], 0.0) for f in range(2)], axis=0
        )
        tendency = dot3(jnp.transpose(change), square[...])
        tend_send[...] = tendency.reshape(n_col, cap, width)

        def give(step, carry):
            other = lax.rem(col + step, n_col)
            pltpu.make_async_remote_copy(
                src_ref=tend_send.at[other], dst_ref=tends.at[sec - 1, col],
                send_sem=tend_send_sem, recv_sem=tend_recv_sem,
                device_id=(sec, other), device_id_type=MESH,
            ).start()
            return carry

        lax.fori_loop(1, n_col, give, 0)
        pltpu.make_async_copy(tend_send.at[col], tends.at[sec - 1, col], tend_recv_sem).start()

        for f in range(2):

            def narrow(z, carry, f=f):
                block[f, z] = plain[f, z].astype(BF16)
                return carry

            lax.fori_loop(0, levels_c, narrow, 0, unroll=2)

    @pl.when(jnp.logical_not(is_cloud))
    def _():
        to_right.wait_recv()
        to_left.wait_recv()
        fetch.wait()

    store = pltpu.make_async_copy(block, new_cloud_ref.at[0], local_sem.at[1])
    store.start()

    around = jnp.concatenate([halo[0], halo[1], own], axis=0)
    spread = rate * pick(near_e, around)
    adv_ref[...] = base
    for k in range(4):
        adv_ref[pl.ds(k, elements, stride=4), :] += spread
    member = jnp.where(
        slot_column == iota((rows, (n_sec - 1) * slots), 1).astype(F32), 1.0, 0.0
    ).astype(BF16)

    def passing(source, step):
        return pltpu.make_async_remote_copy(
            src_ref=tends.at[source], dst_ref=tends.at[source],
            send_sem=group_send_sem.at[step], recv_sem=group_recv_sem.at[source],
            device_id=(lax.rem(sec + step, n_sec), col), device_id_type=MESH,
        )

    @pl.when(is_cloud)
    def _():
        pltpu.make_async_copy(tends.at[sec - 1], tends.at[sec - 1], tend_recv_sem).wait()
        for step in range(1, n_sec):
            passing(sec - 1, step).start()

    for source in range(n_sec - 1):

        @pl.when(sec != source + 1)
        def _():
            passing(source, 1).wait_recv()

    gathered = tends[...].reshape((n_sec - 1) * slots, width)
    summed = adv_ref[...] + pick(member, gathered)
    out_ref[...] = jnp.where(
        iota((rows, width), 1) >= levels_h, jnp.maximum(summed, 0.0), summed
    )

    to_right.wait_send()
    to_left.wait_send()
    store.wait()

    @pl.when(is_cloud)
    def _():
        others = pl.ds(0, n_col - 1)
        pltpu.make_async_copy(disp_send.at[others], disp_send.at[others], disp_send_sem).wait()
        pltpu.make_async_copy(tend_send.at[others], tend_send.at[others], tend_send_sem).wait()
        for step in range(1, n_sec):
            passing(sec - 1, step).wait_send()


def body(
    column_state, mixing_rate, neighbours, assignment, substeps, cloud_state, level_map, saturation
):
    n_sec, n_col = lax.axis_size("sec"), lax.axis_size("col")
    rows, width = column_state.shape
    elements = rows // 4
    _, fields, levels_c, across, slots = cloud_state.shape
    cap, levels_h = slots // n_col, level_map.shape[1]
    vmem = pl.BlockSpec(memory_space=pltpu.VMEM)
    hbm = pl.BlockSpec(memory_space=pl.ANY)
    message = (n_col, cap, width)
    dma = pltpu.SemaphoreType.DMA
    return pl.pallas_call(
        functools.partial(kernel, (n_sec, n_col)),
        out_shape=(
            jax.ShapeDtypeStruct(column_state.shape, F32),
            jax.ShapeDtypeStruct(cloud_state.shape, BF16),
        ),
        in_specs=[vmem, vmem, vmem, vmem, vmem, hbm, vmem, pl.BlockSpec(memory_space=pltpu.SMEM)],
        out_specs=(vmem, hbm),
        scratch_shapes=[
            pltpu.VMEM((fields, levels_c, across, slots), BF16),
            pltpu.VMEM((fields, levels_c, across, slots), F32),
            pltpu.VMEM((fields, levels_c, across, slots), F32),
            pltpu.VMEM((fields, levels_h, 8, slots), F32),
            pltpu.VMEM((fields, levels_h, slots), F32),
            pltpu.VMEM((fields * levels_h, fields * levels_h), F32),
            pltpu.VMEM((elements, width), F32),
            pltpu.VMEM((2, elements, width), F32),
            pltpu.VMEM(message, F32),
            pltpu.VMEM(message, F32),
            pltpu.VMEM(message, F32),
            pltpu.VMEM((n_sec - 1,) + message, F32),
            pltpu.VMEM((rows, width), F32),
            dma((2,)),
            dma((2,)),
            dma((2,)),
            dma,
            dma,
            dma,
            dma,
            dma((n_sec,)),
            dma((n_sec - 1,)),
        ],
        compiler_params=pltpu.CompilerParams(
            collective_id=0, has_side_effects=True, vmem_limit_bytes=48 * 1024 * 1024
        ),
    )(
        column_state,
        mixing_rate.reshape(1, width),
        neighbours.T,
        assignment.reshape(1, rows),
        substeps.reshape(1, rows),
        cloud_state,
        level_map,
        saturation,
    )


def solution(mesh):
    in_specs = (
        P("col", None),
        P(),
        P("col", None),
        P("col", None),
        P("col"),
        P("sec", None, None, None, "col"),
        P(),
        P(),
    )
    out_specs = (P("col", None), P("sec", None, None, None, "col"))
    return jax.shard_map(body, mesh=mesh, in_specs=in_specs, out_specs=out_specs, check_vma=False)
```

time: 144 us -> 47.6 us (0.33)
  waiting for transfers between devices: 59.5 us -> 0 us
  Pallas kernels: 0 us -> 41.6 us
  starting transfers between devices: 31.7 us -> 0 us
  other arithmetic: 21 us -> 0 us
  between operations: 14.7 us -> 0.69 us
  local copies, waits for them, and re-layouts: 15.8 us -> 5.13 us
    pallas_call x0 -> x1, Pallas kernels: none -> 41.6 us  [body(): pl.pallas_call(functools.partial(kernel, (n_sec, n_col)), out_shape=(jax....]
    psum x1 -> x0, waiting for transfers between devices: 32.9 us -> none  [body(): summed = lax.psum(contribution, 'sec')]
    all_to_all x3 -> x0, waiting for transfers between devices: 26.6 us -> none  [the longest x1 10.9 us: body(): lax.all_to_all(tendency, 'col', split_axis=0, concat_axis=0, tiled=True)]
    all_to_all x3 -> x0, starting transfers between devices: 20.3 us -> none  [the longest x1 9.47 us: body(): lax.all_to_all(out_counts, 'col', split_axis=0, concat_axis=0, tiled=True)]
    ppermute x2 -> x0, starting transfers between devices: 11.4 us -> none  [the longest x1 11.4 us: extended_2(): lax.ppermute(head, axis, [((i + 1) % count, i) for i in range(count)])]
    add x14 -> x0, other arithmetic: 7.92 us -> none  [the longest x4 5.53 us: cloud_substep(): fields = fields + HORIZ * across + VERTIC * (upper + lower - 2.0 * fields)]
    slice x18 -> x0, local copies, waits for them, and re-layouts: 4.64 us -> none  [the longest x8 2.63 us: cloud_substep(): jnp.roll(fields, -1, axis=2)]
    convert_element_type x1 -> x0, other arithmetic: 4.56 us -> none  [run_cloud(): return (fields.astype(jnp.bfloat16), tendency)]
  transfers between devices with their start and end apart: 6 -> 0, of which waited for: 4 -> 0; matrix products, arithmetic and copies ran while one was open for 11% -> 0% of each run, Pallas kernels for 0% -> 0%
where the time goes in v1:
time: 47.6 us; the launch traced here: 47.4 us
  Pallas kernels  41.6 us (87%)
  local copies, waits for them, and re-layouts  5.13 us (11%)
  between operations  0.69 us (1%)
    pallas_call x1, Pallas kernels, body(): pl.pallas_call(functools.partial(kernel, (n_sec, n_col)), out_shape=(jax....  41.6 us
    unnamed x18, local copies, waits for them, and re-layouts  5.13 us

profile of v1, /device:TPU:1, one launch (start us, length us, event | category | flops | bytes accessed | tf_op | source)
XLA Modules:
  0.0 47.4 jit_solution(15989801224170919109)
XLA Ops:
  0.6 0.0 copy-start.5
  0.6 0.0 copy-start.7
  0.7 0.0 copy-start.3
  0.7 0.0 copy-start.4
  0.7 0.0 copy-start.6
  0.7 0.6 %copy-done.5 = s32[256]{0:T(256)S(1)} copy-done((s32[256]{0:T(256)S(1)}, s32[256]{0:T(256)}, u32[]{:S(2)}) %copy-start.5) | copy-done | bytes 1048
  1.3 0.0 copy-done.7
  1.3 0.0 copy-done.3
  1.3 0.0 copy-done.4
  1.4 0.0 copy-done.6
  1.4 0.0 copy-start
  1.4 1.2 %copy-done = bf16[1,2,58,32,128]{4,3,2,1,0:T(8,128)(2,1)S(1)} copy-done((bf16[1,2,58,32,128]{4,3,2,1,0:T(8,128)(2,1)S(1)}, bf16[1,2,58,32,128]{4,3,2,1,0:T(8,128)(2,1)}, u32[]{:S(2)}) %copy-start) | copy-done | bytes 950296
  2.6 0.0 copy-start.1
  2.6 0.9 %copy-done.1 = f32[256,128]{1,0:T(8,128)S(1)} copy-done((f32[256,128]{1,0:T(8,128)S(1)}, f32[256,128]{1,0:T(8,128)}, u32[]{:S(2)}) %copy-start.1) | copy-done | bytes 131096
  3.5 0.0 copy-start.2
  3.5 0.8 %copy-done.2 = f32[58,64]{1,0:T(8,128)S(1)} copy-done((f32[58,64]{1,0:T(8,128)S(1)}, f32[58,64]{1,0:T(8,128)}, u32[]{:S(2)}) %copy-start.2) | copy-done | bytes 14872
  4.2 41.6 %shard_map.95 = (f32[256,128]{1,0:T(8,128)S(1)}, bf16[1,2,58,32,128]{4,3,2,1,0:T(8,128)(2,1)S(1)}) custom-call(f32[256,128]{1,0:T(8,128)S(1)} %copy-done.1, f32[1,128]{1,0:T(1,128)S(1)} %bitcast.7, s32[4,64]{1,0:T(4,128)S(1)} %bitcast.4, s32[1,256]{1,0:T(1,128)S(1)} %bitcast.5, s32[1,256]{1,0:T(1,128)S(1)} %bitcast.6, ...), custom_call_target="tpu_custom_call" | custom-call | tf_op jit(solution)/shard_map/pallas_call | solution.py:424
  45.8 0.7 %copy.12 = f32[256,128]{1,0:T(8,128)} copy(f32[256,128]{1,0:T(8,128)S(1)} %get-tuple-element.4) | data formatting | bytes 262144
  46.5 0.9 %copy.13 = bf16[1,2,58,32,128]{4,3,2,1,0:T(8,128)(2,1)} copy(bf16[1,2,58,32,128]{4,3,2,1,0:T(8,128)(2,1)S(1)} %get-tuple-element.5) | data formatting | bytes 1900544
Async XLA Ops:
  0.6 0.7 %copy-start.5 = (s32[256]{0:T(256)S(1)}, s32[256]{0:T(256)}, u32[]{:S(2)}) copy-start(s32[256]{0:T(256)} %param.12) | copy-start | bytes 3076
  0.6 0.7 %copy-start.7 = (f32[58]{0:T(128)S(1)}, f32[58]{0:T(128)}, u32[]{:S(2)}) copy-start(f32[58]{0:T(128)} %sat_ref.1) | copy-start | bytes 700
  0.7 0.7 %copy-start.3 = (s32[64,4]{0,1:T(4,128)S(1)}, s32[64,4]{0,1:T(4,128)}, u32[]{:S(2)}) copy-start(s32[64,4]{0,1:T(4,128)} %param.10) | copy-start | bytes 3076
  0.7 0.7 %copy-start.4 = (s32[256,1]{0,1:T(1,128)S(1)}, s32[256,1]{0,1:T(1,128)}, u32[]{:S(2)}) copy-start(s32[256,1]{0,1:T(1,128)} %param.11) | copy-start | bytes 3076
  0.7 0.7 %copy-start.6 = (f32[128]{0:T(128)S(1)}, f32[128]{0:T(128)}, u32[]{:S(2)}) copy-start(f32[128]{0:T(128)} %param.9) | copy-start | bytes 1540
  1.4 1.2 %copy-start = (bf16[1,2,58,32,128]{4,3,2,1,0:T(8,128)(2,1)S(1)}, bf16[1,2,58,32,128]{4,3,2,1,0:T(8,128)(2,1)}, u32[]{:S(2)}) copy-start(bf16[1,2,58,32,128]{4,3,2,1,0:T(8,128)(2,1)} %cloud_ref.1) | copy-start | bytes 2850820
  2.6 0.9 %copy-start.1 = (f32[256,128]{1,0:T(8,128)S(1)}, f32[256,128]{1,0:T(8,128)}, u32[]{:S(2)}) copy-start(f32[256,128]{1,0:T(8,128)} %cs_ref.1) | copy-start | bytes 393220
  3.5 0.8 %copy-start.2 = (f32[58,64]{1,0:T(8,128)S(1)}, f32[58,64]{1,0:T(8,128)}, u32[]{:S(2)}) copy-start(f32[58,64]{1,0:T(8,128)} %map_ref.1) | copy-start | bytes 44548

commit v2 on v1

v2 whole, which is shorter than its diff:
```python
import functools

import jax
import jax.numpy as jnp
from jax import lax
from jax.experimental import pallas as pl
from jax.experimental.pallas import tpu as pltpu
from jax.sharding import PartitionSpec as P

MAX_SUB = 4
RELAX = 0.25
HORIZ = 0.12
VERTIC = 0.1
LATENT = 2.5
VMIX = 0.2
UNROLL = 29
CENTRE = 1.0 - 2.0 * HORIZ - 2.0 * VERTIC
MESH = pl.DeviceIdType.MESH
F32 = jnp.float32
BF16 = jnp.bfloat16
I32 = jnp.int32
NN = (((1,), (0,)), ((), ()))
NT = (((1,), (1,)), ((), ()))
ACROSS = ((2, 1), (1, 1), (3, 1), (2, 0), (0, 1), (1, 0), (3, 0), (0, 0))


def iota(shape, dim):
    return lax.broadcasted_iota(I32, shape, dim)


def halves(x):
    hi = x.astype(BF16)
    return hi, (x - hi.astype(F32)).astype(BF16)


def dot(a, b, dims=NN):
    return lax.dot_general(a, b, dims, preferred_element_type=F32)


def pick(exact, x, dims=NN):
    hi, lo = halves(x)
    return dot(exact, hi, dims) + dot(exact, lo, dims)


def dot3(x, y, dims=NN):
    xh, xl = halves(x)
    yh, yl = halves(y)
    return dot(xh, yh, dims) + (dot(xh, yl, dims) + dot(xl, yh, dims))


def for_others(col, visit):
    y, x, z = col // 16, lax.rem(col // 8, 2), lax.rem(col, 8)
    bases = [lax.rem(y + dy, 4) * 16 + lax.rem(x + dx, 2) * 8 for dy, dx in ACROSS]

    def ring(t, carry):
        half = (t + 1) // 2
        dz = 4 + half - 2 * half * lax.rem(t, 2)
        along = lax.rem(z + dz, 8)
        for base in bases:
            visit(base + along)
        return carry

    lax.fori_loop(0, 7, ring, 0)
    for base in bases[:-1]:
        visit(base + z)


def kernel(
    sizes,
    cs_hbm,
    rate_hbm,
    nbr_hbm,
    asg_hbm,
    cnt_hbm,
    cloud_hbm,
    map_hbm,
    sat_hbm,
    out_ref,
    block,
    cs_ref,
    rate_ref,
    nbr_ref,
    asg_ref,
    cnt_ref,
    map_ref,
    sat_ref,
    plain_energy,
    plain_water,
    energy_a,
    energy_b,
    water_a,
    water_b,
    drops,
    parts,
    limits,
    offsets,
    square,
    means,
    halo,
    disp_send,
    disp_recv,
    tend_send,
    tends,
    adv_ref,
    local_sem,
    halo_send_sem,
    halo_recv_sem,
    relay_sem,
    disp_send_sem,
    disp_recv_sem,
    tend_send_sem,
    tend_recv_sem,
    core_send_sem,
    core_recv_sem,
):
    n_sec, n_col = sizes
    sec, col = lax.axis_index("sec"), lax.axis_index("col")
    rows, width = cs_ref.shape
    elements = rows // 4
    total = elements * n_col
    cap, slots = disp_send.shape[1], n_col * disp_send.shape[1]
    levels_c, levels_h = map_ref.shape
    left, right = lax.rem(col + n_col - 1, n_col), lax.rem(col + 1, n_col)
    is_cloud = sec > 0
    plain = (plain_energy, plain_water)
    across = plain_water.shape[1]
    core = lax.rem(sec, 2)
    sibling = sec + 1 - 2 * core
    facing = lax.rem(sec + 2, n_sec)

    fetches = [
        pltpu.make_async_copy(src, dst, local_sem.at[i])
        for i, (src, dst) in enumerate(
            (
                (cs_hbm, cs_ref),
                (asg_hbm, asg_ref),
                (nbr_hbm, nbr_ref),
                (rate_hbm, rate_ref),
                (map_hbm, map_ref),
                (cnt_hbm, cnt_ref),
                (sat_hbm, sat_ref),
                (cloud_hbm, block),
            )
        )
    ]
    for fetch in fetches:
        fetch.start()

    barrier = pltpu.get_barrier_semaphore()

    def greet(device):
        pl.semaphore_signal(barrier, inc=1, device_id=device, device_id_type=MESH)

    greet((0, left))
    greet((0, right))

    @pl.when(is_cloud)
    def _():
        for_others(col, lambda other: greet((sec, other)))

    greet((sibling, col))

    @pl.when(sec != 2)
    def _():
        greet((facing, col))

    fetches[0].wait()
    own = (
        cs_ref[pl.ds(0, elements, stride=4), :]
        + cs_ref[pl.ds(1, elements, stride=4), :]
        + cs_ref[pl.ds(2, elements, stride=4), :]
        + cs_ref[pl.ds(3, elements, stride=4), :]
    ) * 0.25
    means[...] = own

    def sharing(section, side):
        return pltpu.make_async_remote_copy(
            src_ref=means, dst_ref=halo.at[side],
            send_sem=halo_send_sem.at[side, section // 2], recv_sem=halo_recv_sem.at[side],
            device_id=(section, (right, left)[side]), device_id_type=MESH,
        )

    def relay(side):
        return pltpu.make_async_remote_copy(
            src_ref=halo.at[side], dst_ref=halo.at[side],
            send_sem=relay_sem.at[side], recv_sem=halo_recv_sem.at[side],
            device_id=(sibling, col), device_id_type=MESH,
        )

    def halo_arrives():
        for side in range(2):
            relay(side).wait_recv()

            @pl.when(core == 0)
            def _():
                relay(side).start()

    @pl.when(jnp.logical_not(is_cloud))
    def _():
        pl.semaphore_wait(barrier, 2 * n_sec + 1)
        for section in (2, 0):
            for side in range(2):
                sharing(section, side).start()

    for fetch in fetches[1:7]:
        fetch.wait()

    asg = asg_ref[...]
    asg_column = jnp.transpose(jnp.broadcast_to(asg.astype(F32), (128, rows)))[:, 0:1]
    same = (asg_column == asg.astype(F32)) & (iota((rows, rows), 0) < iota((rows, rows), 1))
    rank = jnp.max(jnp.where(same, 1.0, 0.0), axis=0, keepdims=True)
    slot = (asg * cap).astype(F32) + rank

    place = iota((3 * elements, elements), 0)
    place = jnp.where(
        place < elements, place, jnp.where(place < 2 * elements, place + elements, place - elements)
    )
    near = jnp.where(place == elements + iota((3 * elements, elements), 1), -4.0, 0.0)
    relative = jnp.bitwise_and(nbr_ref[...] - (col - 1) * elements, total - 1)
    for k in range(4):
        near = near + jnp.where(relative[k : k + 1, :] == place, 1.0, 0.0)
    near_t = near.astype(BF16)

    cs = cs_ref[...]
    lane = jnp.bitwise_and(iota((rows, width), 1), levels_h - 1)
    upper = jnp.where(lane == levels_h - 1, cs, pltpu.roll(cs, width - 1, axis=1))
    lower = jnp.where(lane == 0, cs, pltpu.roll(cs, 1, axis=1))
    base = cs + VMIX * (upper + lower - 2.0 * cs)
    rate = rate_ref[...]

    square[...] = jnp.zeros_like(square)
    square[0:levels_c, 0:levels_h] = map_ref[...]
    square[levels_h : levels_h + levels_c, levels_h : 2 * levels_h] = map_ref[...]

    @pl.when(is_cloud)
    def _():
        chosen = iota((slots, rows), 0) + (sec - 1) * slots == slot.astype(I32)
        chosen32 = jnp.where(chosen, 1.0, 0.0)
        chosen16 = chosen32.astype(BF16)
        counts_out = jnp.sum(chosen32 * cnt_ref[...].astype(F32), axis=1, keepdims=True)
        repeat = jnp.where(
            iota((elements, rows), 0) == lax.shift_right_logical(iota((elements, rows), 1), 2), 1.0, 0.0
        ).astype(BF16)
        by_element = dot(chosen16, repeat, NT).astype(BF16)
        reach = dot(by_element, near_t, NT).astype(BF16)
        known = pick(chosen16, base) + rate * pick(reach[:, 2 * elements :], own)
        reach = reach[:, : 2 * elements]

        halo_arrives()
        outside = halo[...].reshape(2 * elements, width)
        sent = known + rate * pick(reach, outside)
        target = dot3(sent, square[...], NT)
        target = jnp.where(iota((slots, width), 1) == levels_c, counts_out, target)
        disp_send[...] = target.reshape(n_col, cap, width)

        pl.semaphore_wait(barrier, n_col + 1)
        def send(other):
            pltpu.make_async_remote_copy(
                src_ref=disp_send.at[other], dst_ref=disp_recv.at[col],
                send_sem=disp_send_sem, recv_sem=disp_recv_sem,
                device_id=(sec, other), device_id_type=MESH,
            ).start()

        for_others(col, send)
        pltpu.make_async_copy(disp_send.at[col], disp_recv.at[col], disp_recv_sem).start()

        fetches[7].wait()
        for f in range(2):
            parts[f, levels_c:] = jnp.zeros((levels_h - levels_c, 8, slots), F32)

            def widen(z, carry, f=f):
                x = block[0, f, z].astype(F32)
                plain[f][z] = x
                parts[f, z] = (x[0:8] + x[8:16]) + (x[16:24] + x[24:32])
                return carry

            lax.fori_loop(0, levels_c, widen, 0, unroll=UNROLL)

        def strided(ref, z):
            return tuple(ref[z, pl.ds(k, 8, stride=4), :] for k in range(4))

        def packed(ref, z):
            return tuple(ref[z, pl.ds(8 * k, 8), :] for k in range(4))

        def put_strided(ref, z, tiles):
            for k in range(4):
                ref[z, pl.ds(k, 8, stride=4), :] = tiles[k]

        def put_packed(ref, z, tiles):
            for k in range(4):
                ref[z, pl.ds(8 * k, 8), :] = tiles[k]

        def stencil(here, below, above, by_x, by_z):
            west = (pltpu.roll(here[3], 1, axis=0),) + here[:3]
            east = here[1:] + (pltpu.roll(here[0], 7, axis=0),)
            return tuple(
                here[k] + (by_x * (east[k] + west[k]) + by_z * (above[k] + below[k]))
                for k in range(4)
            )

        for f in range(2):

            def first(z, carry, f=f):
                below, here = carry
                above = strided(plain[f], jnp.minimum(z + 1, levels_c - 1))
                put_packed(
                    (energy_a, water_a)[f], z, stencil(here, below, above, HORIZ / CENTRE, VERTIC / CENTRE)
                )
                return here, above

            edge = strided(plain[f], 0)
            lax.fori_loop(0, levels_c, first, (edge, edge), unroll=UNROLL)

        columns_inv = 1.0 / across
        start = [jnp.sum(parts[f], axis=1) * columns_inv for f in range(2)]
        level = iota((levels_h, slots), 0)
        wet = jnp.concatenate([sat_ref[...], jnp.zeros((1, 128 - levels_c), F32)], axis=1)
        wet = jnp.transpose(jnp.broadcast_to(wet, (128, 128)))[:levels_h]

        def smoothed(x):
            up = jnp.where(level == levels_c - 1, x, pltpu.roll(x, levels_h - 1, axis=0))
            low = jnp.where(level == 0, x, pltpu.roll(x, 1, axis=0))
            return (1.0 - 2.0 * VERTIC) * x + VERTIC * (up + low)

        pltpu.make_async_copy(disp_recv, disp_recv, disp_recv_sem).wait()
        arrived = jnp.transpose(disp_recv[...].reshape(slots, width))
        counts = arrived[levels_c : levels_c + 1, :]
        counts8 = jnp.broadcast_to(counts, (8, slots))
        goal = [arrived[f * levels_h : (f + 1) * levels_h] for f in range(2)]
        mean = list(start)
        offset = [jnp.zeros((levels_h, slots), F32)] * 2

        for n in range(MAX_SUB):
            scale = CENTRE ** (n + 1)
            keep = counts > float(n)
            moved, shifted = [], []
            for f in range(2):
                d = RELAX * (goal[f] - mean[f])
                moved.append(smoothed(mean[f] + d))
                shifted.append(smoothed(offset[f] + d))
            limit = (0.5 / scale) * (wet - shifted[1])
            limits[...] = limit if n == 0 else jnp.where(keep, limit, 0.0)

            def condense(water, z, by_half):
                bound = jnp.broadcast_to(limits[pl.ds(z, 1), :], (8, slots))
                drop = [jnp.maximum(by_half * water[k] - bound, 0.0) for k in range(4)]
                parts[1, z] = (drop[0] + drop[1]) + (drop[2] + drop[3])
                return [water[k] - drop[k] for k in range(4)], drop

            if n == 0:

                def finish(z, carry):
                    new, drop = condense(packed(water_a, z), z, 0.5)
                    put_packed(water_b, z, new)
                    put_packed(drops.at[0], z, drop)
                    return carry

                lax.fori_loop(0, levels_c, finish, 0, unroll=UNROLL)
            else:
                going = jnp.where(counts8 > float(n), 1.0, 0.0)
                by_x, by_z, by_half = going * (HORIZ / CENTRE), going * (VERTIC / CENTRE), going * 0.5
                old, fresh = (water_b, water_a) if n % 2 else (water_a, water_b)

                def sweep(z, carry, n=n, old=old, fresh=fresh, by_x=by_x, by_z=by_z, by_half=by_half):
                    below, here = carry
                    above = packed(old, jnp.minimum(z + 1, levels_c - 1))
                    new, drop = condense(stencil(here, below, above, by_x, by_z), z, by_half)
                    if n == MAX_SUB - 1:
                        put_strided(plain_water, z, new)
                        put_strided(drops.at[n], z, drop)
                    else:
                        put_packed(fresh, z, new)
                        put_packed(drops.at[n], z, drop)
                    return here, above

                edge = packed(old, 0)
                lax.fori_loop(0, levels_c, sweep, (edge, edge), unroll=UNROLL)

            dried = jnp.sum(parts[1], axis=1) * (columns_inv * scale)
            mean[0] = jnp.where(keep, moved[0] + LATENT * dried, mean[0])
            mean[1] = jnp.where(keep, moved[1] - dried, mean[1])
            offset = [jnp.where(keep, shifted[f], offset[f]) for f in range(2)]

        change = jnp.concatenate(
            [jnp.where(level < levels_c, mean[f] - start[f], 0.0) for f in range(2)], axis=0
        )
        tendency = dot3(jnp.transpose(change), square[...])
        tend_send[...] = tendency.reshape(n_col, cap, width)

        def give(other, chip):
            pltpu.make_async_remote_copy(
                src_ref=tend_send.at[other], dst_ref=tends.at[sec - 1, col],
                send_sem=tend_send_sem.at[chip], recv_sem=tend_recv_sem.at[sec - 1],
                device_id=((sec, facing)[chip], other), device_id_type=MESH,
            ).start()

        def give_both(other):
            give(other, 1)
            give(other, 0)

        for_others(col, give_both)
        give(col, 1)
        pltpu.make_async_copy(tend_send.at[col], tends.at[sec - 1, col], tend_recv_sem.at[sec - 1]).start()

        for n in range(1, MAX_SUB):
            going = jnp.where(counts8 > float(n), 1.0, 0.0)
            by_x, by_z = going * (HORIZ / CENTRE), going * (VERTIC / CENTRE)

            old, fresh = (energy_a, energy_b) if n % 2 else (energy_b, energy_a)

            def warmed(z, n=n, old=old):
                energy, drop = packed(old, z), packed(drops.at[n - 1], z)
                return tuple(energy[k] + LATENT * drop[k] for k in range(4))

            def follow(z, carry, n=n, fresh=fresh, by_x=by_x, by_z=by_z, warmed=warmed):
                below, here = carry
                above = warmed(jnp.minimum(z + 1, levels_c - 1))
                new = stencil(here, below, above, by_x, by_z)
                if n == MAX_SUB - 1:
                    put_strided(plain_energy, z, new)
                else:
                    put_packed(fresh, z, new)
                return here, above

            edge = warmed(0)
            lax.fori_loop(0, levels_c, follow, (edge, edge), unroll=UNROLL)

        power = jnp.full((1, slots), CENTRE, F32)
        for n in range(1, MAX_SUB):
            power = jnp.where(counts > float(n), CENTRE ** (n + 1), power)
        used = jnp.broadcast_to(counts, (across, slots)) > 0.0
        power = jnp.broadcast_to(power, (across, slots))
        for f in range(2):
            offsets[f] = offset[f]

            def narrow(z, carry, f=f):
                x = plain[f][z]
                if f == 0:
                    x = x + LATENT * drops[MAX_SUB - 1, z]
                x = power * x + jnp.broadcast_to(offsets[f, pl.ds(z, 1), :], x.shape)
                block[0, f, z] = jnp.where(used, x, block[0, f, z].astype(F32)).astype(BF16)
                return carry

            lax.fori_loop(0, levels_c, narrow, 0, unroll=UNROLL)

    @pl.when(jnp.logical_not(is_cloud))
    def _():
        halo_arrives()
        fetches[7].wait()

    near_e = jnp.transpose(
        jnp.concatenate([near, jnp.zeros((3 * elements, 128 - elements), F32)], axis=1)
    )[:elements].astype(BF16)
    around = jnp.concatenate([halo[0], halo[1], own], axis=0)
    spread = rate * pick(near_e, around)
    adv_ref[...] = base
    for k in range(4):
        adv_ref[pl.ds(k, elements, stride=4), :] += spread
    slot_column = jnp.transpose(jnp.broadcast_to(slot, (128, rows)))[:, 0:1]
    member = jnp.where(
        slot_column == iota((rows, (n_sec - 1) * slots), 1).astype(F32), 1.0, 0.0
    ).astype(BF16)

    def heard(source):
        pltpu.make_async_copy(tends.at[source], tends.at[source], tend_recv_sem.at[source]).wait()

    def passing(source):
        return pltpu.make_async_remote_copy(
            src_ref=tends.at[source], dst_ref=tends.at[source],
            send_sem=core_send_sem.at[source], recv_sem=core_recv_sem.at[source],
            device_id=(sibling, col), device_id_type=MESH,
        )

    def gather(sources):
        for source in sources:
            found = tends[source].reshape(slots, width)
            adv_ref[...] += pick(member[:, source * slots : (source + 1) * slots], found)

    for mine, theirs in (((1,), (0, 2)), ((0, 2), (1,))):

        @pl.when(core == len(mine) - 1)
        def _():
            for source in mine:
                heard(source)
                passing(source).start()
            gather(mine)
            for source in theirs:
                passing(source).wait_recv()
            gather(theirs)

    summed = adv_ref[...]
    out_ref[...] = jnp.where(
        iota((rows, width), 1) >= levels_h, jnp.maximum(summed, 0.0), summed
    )

    @pl.when(jnp.logical_not(is_cloud))
    def _():
        for section in (2, 0):
            for side in range(2):
                sharing(section, side).wait_send()

    @pl.when(core == 0)
    def _():
        for side in range(2):
            relay(side).wait_send()

    for mine in ((1,), (0, 2)):

        @pl.when(core == len(mine) - 1)
        def _():
            for source in mine:
                passing(source).wait_send()

    @pl.when(is_cloud)
    def _():
        others = pl.ds(0, n_col - 1)
        pltpu.make_async_copy(disp_send.at[others], disp_send.at[others], disp_send_sem).wait()
        pltpu.make_async_copy(tend_send.at[others], tend_send.at[others], tend_send_sem.at[0]).wait()
        pltpu.make_async_copy(tend_send, tend_send, tend_send_sem.at[1]).wait()


def body(
    column_state, mixing_rate, neighbours, assignment, substeps, cloud_state, level_map, saturation
):
    n_sec, n_col = lax.axis_size("sec"), lax.axis_size("col")
    rows, width = column_state.shape
    elements = rows // 4
    _, fields, levels_c, across, slots = cloud_state.shape
    cap, levels_h = slots // n_col, level_map.shape[1]
    vmem = pl.BlockSpec(memory_space=pltpu.VMEM)
    hbm = pl.BlockSpec(memory_space=pltpu.HBM)
    message = (n_col, cap, width)
    dma = pltpu.SemaphoreType.DMA
    results = (
        jax.ShapeDtypeStruct(column_state.shape, F32),
        jax.ShapeDtypeStruct(cloud_state.shape, BF16),
    )
    operands = (
        column_state,
        mixing_rate.reshape(1, width),
        neighbours.T,
        assignment.reshape(1, rows),
        substeps.reshape(1, rows),
        cloud_state,
        level_map,
        saturation.reshape(1, levels_c),
    )
    return pl.pallas_call(
        functools.partial(kernel, (n_sec, n_col)),
        out_shape=tuple(pltpu.VMEM(r.shape, r.dtype) for r in results),
        in_specs=[hbm] * 8,
        out_specs=(vmem, vmem),
        scratch_shapes=[
            pltpu.VMEM((rows, width), F32),
            pltpu.VMEM((1, width), F32),
            pltpu.VMEM((4, elements), I32),
            pltpu.VMEM((1, rows), I32),
            pltpu.VMEM((1, rows), I32),
            pltpu.VMEM((levels_c, levels_h), F32),
            pltpu.VMEM((1, levels_c), F32),
            *[pltpu.VMEM((levels_c, across, slots), F32)] * 6,
            pltpu.VMEM((MAX_SUB, levels_c, across, slots), F32),
            pltpu.VMEM((fields, levels_h, 8, slots), F32),
            pltpu.VMEM((levels_h, slots), F32),
            pltpu.VMEM((fields, levels_h, slots), F32),
            pltpu.VMEM((fields * levels_h, fields * levels_h), F32),
            pltpu.VMEM((elements, width), F32),
            pltpu.VMEM((2, elements, width), F32),
            pltpu.VMEM(message, F32),
            pltpu.VMEM(message, F32),
            pltpu.VMEM(message, F32),
            pltpu.VMEM((n_sec - 1,) + message, F32),
            pltpu.VMEM((rows, width), F32),
            dma((8,)),
            dma((2, 2)),
            dma((2,)),
            dma((2,)),
            dma,
            dma,
            dma((2,)),
            dma((n_sec - 1,)),
            dma((n_sec - 1,)),
            dma((n_sec - 1,)),
        ],
        compiler_params=pltpu.CompilerParams(
            collective_id=0, has_side_effects=True, vmem_limit_bytes=48 * 1024 * 1024
        ),
    )(*(pltpu.with_memory_space_constraint(x, pltpu.HBM) for x in operands))


def solution(mesh):
    in_specs = (
        P("col", None),
        P(),
        P("col", None),
        P("col", None),
        P("col"),
        P("sec", None, None, None, "col"),
        P(),
        P(),
    )
    out_specs = (P("col", None), P("sec", None, None, None, "col"))
    return jax.shard_map(body, mesh=mesh, in_specs=in_specs, out_specs=out_specs, check_vma=False)
```

time: 47.6 us -> 37.2 us (0.78)
  Pallas kernels: 41.6 us -> 34.9 us
  local copies, waits for them, and re-layouts: 5.13 us -> 1.59 us
    pallas_call x1, Pallas kernels: 41.6 us -> 34.9 us  [body(): pl.pallas_call(functools.partial(kernel, (n_sec, n_col)), out_shape=tuple...]
    unnamed x18 -> x2, local copies, waits for them, and re-layouts: 5.13 us -> 1.59 us
where the time goes in v2:
time: 37.2 us; the launch traced here: 37.1 us
  Pallas kernels  34.9 us (94%)
  local copies, waits for them, and re-layouts  1.59 us (4%)
  between operations  0.64 us (2%)
    pallas_call x1, Pallas kernels, body(): pl.pallas_call(functools.partial(kernel, (n_sec, n_col)), out_shape=tuple...  34.9 us
    unnamed x2, local copies, waits for them, and re-layouts  1.59 us

profile of v2, /device:TPU:1, one launch (start us, length us, event | category | flops | bytes accessed | tf_op | source)
XLA Modules:
  0.0 37.1 jit_solution(4211456032021060538)
XLA Ops:
  0.6 34.9 %shard_map.95 = (f32[256,128]{1,0:T(8,128)S(1)}, bf16[1,2,58,32,128]{4,3,2,1,0:T(8,128)(2,1)S(1)}) custom-call(f32[256,128]{1,0:T(8,128)} %cs_hbm.1, f32[1,128]{1,0:T(1,128)} %bitcast.8, s32[4,64]{1,0:T(4,128)} %bitcast.5, s32[1,256]{1,0:T(1,128)} %bitcast.6, s32[1,256]{1,0:T(1,128)} %bitcast.7, bf16[1,2,58,32,128]{4,3,2,1,0:T(8,128)(2,1)} %cloud_hbm.1, ...), custom_call_target="tpu_custom_call" | custom-call | tf_op jit(solution)/shard_map/pallas_call | solution.py:548
  35.6 0.7 %copy.12 = f32[256,128]{1,0:T(8,128)} copy(f32[256,128]{1,0:T(8,128)S(1)} %get-tuple-element.2) | data formatting | bytes 262144
  36.2 0.9 %copy.13 = bf16[1,2,58,32,128]{4,3,2,1,0:T(8,128)(2,1)} copy(bf16[1,2,58,32,128]{4,3,2,1,0:T(8,128)(2,1)S(1)} %get-tuple-element.3) | data formatting | bytes 1900544

commit v3 on v2

--- a/solution.py
+++ b/solution.py
@@ -95,17 +95,19 @@
     limits,
     offsets,
     square,
-    means,
-    halo,
+    pushed,
+    given,
+    beyond,
     disp_send,
     disp_recv,
     tend_send,
     tends,
     adv_ref,
     local_sem,
-    halo_send_sem,
-    halo_recv_sem,
+    push_send_sem,
+    push_recv_sem,
     relay_sem,
+    beyond_sem,
     disp_send_sem,
     disp_recv_sem,
     tend_send_sem,
@@ -152,7 +154,6 @@
         pl.semaphore_signal(barrier, inc=1, device_id=device, device_id_type=MESH)
 
     greet((0, left))
-    greet((0, right))
 
     @pl.when(is_cloud)
     def _():
@@ -171,45 +172,54 @@
         + cs_ref[pl.ds(2, elements, stride=4), :]
         + cs_ref[pl.ds(3, elements, stride=4), :]
     ) * 0.25
-    means[...] = own
-
-    def sharing(section, side):
-        return pltpu.make_async_remote_copy(
-            src_ref=means, dst_ref=halo.at[side],
-            send_sem=halo_send_sem.at[side, section // 2], recv_sem=halo_recv_sem.at[side],
-            device_id=(section, (right, left)[side]), device_id_type=MESH,
-        )
-
-    def relay(side):
-        return pltpu.make_async_remote_copy(
-            src_ref=halo.at[side], dst_ref=halo.at[side],
-            send_sem=relay_sem.at[side], recv_sem=halo_recv_sem.at[side],
-            device_id=(sibling, col), device_id_type=MESH,
-        )
-
-    def halo_arrives():
-        for side in range(2):
-            relay(side).wait_recv()
-
-            @pl.when(core == 0)
-            def _():
-                relay(side).start()
-
-    @pl.when(jnp.logical_not(is_cloud))
-    def _():
-        pl.semaphore_wait(barrier, 2 * n_sec + 1)
-        for section in (2, 0):
-            for side in range(2):
-                sharing(section, side).start()
-
-    for fetch in fetches[1:7]:
-        fetch.wait()
+    pushed[0:elements] = own
+    fetches[1].wait()
+    fetches[2].wait()
 
     asg = asg_ref[...]
     asg_column = jnp.transpose(jnp.broadcast_to(asg.astype(F32), (128, rows)))[:, 0:1]
     same = (asg_column == asg.astype(F32)) & (iota((rows, rows), 0) < iota((rows, rows), 1))
     rank = jnp.max(jnp.where(same, 1.0, 0.0), axis=0, keepdims=True)
     slot = (asg * cap).astype(F32) + rank
+
+    pushed[elements : elements + 4, 0:elements] = nbr_ref[...].astype(F32)
+    pushed[elements + 4 : elements + 5] = slot[:, :width]
+    pushed[elements + 5 : elements + 6] = slot[:, width:]
+
+    def push(section):
+        return pltpu.make_async_remote_copy(
+            src_ref=pushed, dst_ref=given,
+            send_sem=push_send_sem.at[section - 1], recv_sem=push_recv_sem,
+            device_id=(section, right), device_id_type=MESH,
+        )
+
+    relays = (sec == 1) | (sec == 2)
+    relay = pltpu.make_async_remote_copy(
+        src_ref=given, dst_ref=given, send_sem=relay_sem, recv_sem=push_recv_sem,
+        device_id=(sibling, col), device_id_type=MESH,
+    )
+
+    def push_arrives():
+        relay.wait_recv()
+
+        @pl.when(relays)
+        def _():
+            relay.start()
+
+    means = pushed.at[pl.ds(0, elements)]
+    to_left = pltpu.make_async_remote_copy(
+        src_ref=means, dst_ref=beyond, send_sem=beyond_sem.at[0], recv_sem=beyond_sem.at[1],
+        device_id=(sec, left), device_id_type=MESH,
+    )
+
+    @pl.when(jnp.logical_not(is_cloud))
+    def _():
+        pl.semaphore_wait(barrier, n_sec + 1)
+        for section in (2, 1):
+            push(section).start()
+
+    for fetch in fetches[3:7]:
+        fetch.wait()
 
     place = iota((3 * elements, elements), 0)
     place = jnp.where(
@@ -244,14 +254,25 @@
         by_element = dot(chosen16, repeat, NT).astype(BF16)
         reach = dot(by_element, near_t, NT).astype(BF16)
         known = pick(chosen16, base) + rate * pick(reach[:, 2 * elements :], own)
-        reach = reach[:, : 2 * elements]
-
-        halo_arrives()
-        outside = halo[...].reshape(2 * elements, width)
-        sent = known + rate * pick(reach, outside)
+        reach = reach[:, :elements]
+
+        push_arrives()
+        sent = known + rate * pick(reach, given[0:elements])
         target = dot3(sent, square[...], NT)
         target = jnp.where(iota((slots, width), 1) == levels_c, counts_out, target)
-        disp_send[...] = target.reshape(n_col, cap, width)
+        disp_send[:, :, 0:width] = target.reshape(n_col, cap, width)
+        slot_left = jnp.concatenate([given[elements + 4 : elements + 5], given[elements + 5 : elements + 6]], axis=1)
+        chosen_left = jnp.where(
+            iota((slots, rows), 0) + (sec - 1) * slots == slot_left.astype(I32), 1.0, 0.0
+        ).astype(BF16)
+        nbr_left = given[elements : elements + 4, 0:elements].astype(I32)
+        here = iota((elements, elements), 0) + col * elements
+        near_left = jnp.zeros((elements, elements), F32)
+        for k in range(4):
+            near_left = near_left + jnp.where(nbr_left[k : k + 1, :] == here, 1.0, 0.0)
+        reach_left = dot(dot(chosen_left, repeat, NT).astype(BF16), near_left.astype(BF16), NT)
+        extra = dot3(rate * pick(reach_left.astype(BF16), own), square[...], NT)
+        disp_send[:, :, width:] = extra.reshape(n_col, cap, width)
 
         pl.semaphore_wait(barrier, n_col + 1)
         def send(other):
@@ -263,6 +284,7 @@
 
         for_others(col, send)
         pltpu.make_async_copy(disp_send.at[col], disp_recv.at[col], disp_recv_sem).start()
+        to_left.start()
 
         fetches[7].wait()
         for f in range(2):
@@ -323,7 +345,10 @@
             return (1.0 - 2.0 * VERTIC) * x + VERTIC * (up + low)
 
         pltpu.make_async_copy(disp_recv, disp_recv, disp_recv_sem).wait()
-        arrived = jnp.transpose(disp_recv[...].reshape(slots, width))
+        later = disp_recv[:, :, width:].reshape(slots, width)
+        arrived = jnp.transpose(
+            disp_recv[:, :, 0:width].reshape(slots, width) + pltpu.roll(later, slots - cap, axis=0)
+        )
         counts = arrived[levels_c : levels_c + 1, :]
         counts8 = jnp.broadcast_to(counts, (8, slots))
         goal = [arrived[f * levels_h : (f + 1) * levels_h] for f in range(2)]
@@ -445,13 +470,15 @@
 
     @pl.when(jnp.logical_not(is_cloud))
     def _():
-        halo_arrives()
+        push_arrives()
+        to_left.start()
         fetches[7].wait()
 
     near_e = jnp.transpose(
         jnp.concatenate([near, jnp.zeros((3 * elements, 128 - elements), F32)], axis=1)
     )[:elements].astype(BF16)
-    around = jnp.concatenate([halo[0], halo[1], own], axis=0)
+    to_left.wait_recv()
+    around = jnp.concatenate([given[0:elements], beyond[...], own], axis=0)
     spread = rate * pick(near_e, around)
     adv_ref[...] = base
     for k in range(4):
@@ -495,14 +522,14 @@
 
     @pl.when(jnp.logical_not(is_cloud))
     def _():
-        for section in (2, 0):
-            for side in range(2):
-                sharing(section, side).wait_send()
-
-    @pl.when(core == 0)
-    def _():
-        for side in range(2):
-            relay(side).wait_send()
+        for section in (2, 1):
+            push(section).wait_send()
+
+    @pl.when(relays)
+    def _():
+        relay.wait_send()
+
+    to_left.wait_send()
 
     for mine in ((1,), (0, 2)):
 
@@ -564,16 +591,18 @@
             pltpu.VMEM((levels_h, slots), F32),
             pltpu.VMEM((fields, levels_h, slots), F32),
             pltpu.VMEM((fields * levels_h, fields * levels_h), F32),
+            pltpu.VMEM((elements + 8, width), F32),
+            pltpu.VMEM((elements + 8, width), F32),
             pltpu.VMEM((elements, width), F32),
-            pltpu.VMEM((2, elements, width), F32),
-            pltpu.VMEM(message, F32),
-            pltpu.VMEM(message, F32),
+            pltpu.VMEM((n_col, cap, 2 * width), F32),
+            pltpu.VMEM((n_col, cap, 2 * width), F32),
             pltpu.VMEM(message, F32),
             pltpu.VMEM((n_sec - 1,) + message, F32),
             pltpu.VMEM((rows, width), F32),
             dma((8,)),
-            dma((2, 2)),
             dma((2,)),
+            dma,
+            dma,
             dma((2,)),
             dma,
             dma,

time: 37.2 us -> 35.4 us (0.952)
  Pallas kernels: 34.9 us -> 33 us
    pallas_call x1, Pallas kernels: 34.9 us -> 33 us  [body(): pl.pallas_call(functools.partial(kernel, (n_sec, n_col)), out_shape=tuple...]
where the time goes in v3:
time: 35.4 us; the launch traced here: 35.3 us
  Pallas kernels  33 us (93%)
  local copies, waits for them, and re-layouts  1.59 us (4%)
  between operations  0.64 us (2%)
    pallas_call x1, Pallas kernels, body(): pl.pallas_call(functools.partial(kernel, (n_sec, n_col)), out_shape=tuple...  33 us
    unnamed x2, local copies, waits for them, and re-layouts  1.59 us

profile of v3, /device:TPU:1, one launch (start us, length us, event | category | flops | bytes accessed | tf_op | source)
XLA Modules:
  0.0 35.3 jit_solution(8641358289914977333)
XLA Ops:
  0.6 33.0 %shard_map.95 = (f32[256,128]{1,0:T(8,128)S(1)}, bf16[1,2,58,32,128]{4,3,2,1,0:T(8,128)(2,1)S(1)}) custom-call(f32[256,128]{1,0:T(8,128)} %cs_hbm.1, f32[1,128]{1,0:T(1,128)} %bitcast.8, s32[4,64]{1,0:T(4,128)} %bitcast.5, s32[1,256]{1,0:T(1,128)} %bitcast.6, s32[1,256]{1,0:T(1,128)} %bitcast.7, bf16[1,2,58,32,128]{4,3,2,1,0:T(8,128)(2,1)} %cloud_hbm.1, ...), custom_call_target="tpu_custom_call" | custom-call | tf_op jit(solution)/shard_map/pallas_call | solution.py:575
  33.7 0.7 %copy.12 = f32[256,128]{1,0:T(8,128)} copy(f32[256,128]{1,0:T(8,128)S(1)} %get-tuple-element.2) | data formatting | bytes 262144
  34.3 0.9 %copy.13 = bf16[1,2,58,32,128]{4,3,2,1,0:T(8,128)(2,1)} copy(bf16[1,2,58,32,128]{4,3,2,1,0:T(8,128)(2,1)S(1)} %get-tuple-element.3) | data formatting | bytes 1900544

commit v4 on v3

--- a/solution.py
+++ b/solution.py
@@ -37,15 +37,24 @@
     return lax.dot_general(a, b, dims, preferred_element_type=F32)
 
 
+def joined(lefts, rights, dims):
+    (left_dims, right_dims), _ = dims
+    return dot(
+        jnp.concatenate(lefts, axis=left_dims[0]), jnp.concatenate(rights, axis=right_dims[0]), dims
+    )
+
+
 def pick(exact, x, dims=NN):
     hi, lo = halves(x)
-    return dot(exact, hi, dims) + dot(exact, lo, dims)
+    if exact.shape[1] % 128:
+        return dot(exact, hi, dims) + dot(exact, lo, dims)
+    return joined([exact, exact], [hi, lo], dims)
 
 
 def dot3(x, y, dims=NN):
     xh, xl = halves(x)
     yh, yl = halves(y)
-    return dot(xh, yh, dims) + (dot(xh, yl, dims) + dot(xl, yh, dims))
+    return joined([xh, xh, xl], [yh, yl, yh], dims)
 
 
 def for_others(col, visit):
@@ -90,7 +99,6 @@
     energy_b,
     water_a,
     water_b,
-    drops,
     parts,
     limits,
     offsets,
@@ -134,9 +142,9 @@
         pltpu.make_async_copy(src, dst, local_sem.at[i])
         for i, (src, dst) in enumerate(
             (
-                (cs_hbm, cs_ref),
                 (asg_hbm, asg_ref),
                 (nbr_hbm, nbr_ref),
+                (cs_hbm, cs_ref),
                 (rate_hbm, rate_ref),
                 (map_hbm, map_ref),
                 (cnt_hbm, cnt_ref),
@@ -166,6 +174,19 @@
         greet((facing, col))
 
     fetches[0].wait()
+    fetches[1].wait()
+
+    asg = asg_ref[...]
+    asg_column = jnp.transpose(jnp.broadcast_to(asg.astype(F32), (128, rows)))[:, 0:1]
+    same = (asg_column == asg.astype(F32)) & (iota((rows, rows), 0) < iota((rows, rows), 1))
+    rank = jnp.max(jnp.where(same, 1.0, 0.0), axis=0, keepdims=True)
+    slot = (asg * cap).astype(F32) + rank
+
+    pushed[elements : elements + 4, 0:elements] = nbr_ref[...].astype(F32)
+    pushed[elements + 4 : elements + 5] = slot[:, :width]
+    pushed[elements + 5 : elements + 6] = slot[:, width:]
+
+    fetches[2].wait()
     own = (
         cs_ref[pl.ds(0, elements, stride=4), :]
         + cs_ref[pl.ds(1, elements, stride=4), :]
@@ -173,18 +194,6 @@
         + cs_ref[pl.ds(3, elements, stride=4), :]
     ) * 0.25
     pushed[0:elements] = own
-    fetches[1].wait()
-    fetches[2].wait()
-
-    asg = asg_ref[...]
-    asg_column = jnp.transpose(jnp.broadcast_to(asg.astype(F32), (128, rows)))[:, 0:1]
-    same = (asg_column == asg.astype(F32)) & (iota((rows, rows), 0) < iota((rows, rows), 1))
-    rank = jnp.max(jnp.where(same, 1.0, 0.0), axis=0, keepdims=True)
-    slot = (asg * cap).astype(F32) + rank
-
-    pushed[elements : elements + 4, 0:elements] = nbr_ref[...].astype(F32)
-    pushed[elements + 4 : elements + 5] = slot[:, :width]
-    pushed[elements + 5 : elements + 6] = slot[:, width:]
 
     def push(section):
         return pltpu.make_async_remote_copy(
@@ -258,9 +267,6 @@
 
         push_arrives()
         sent = known + rate * pick(reach, given[0:elements])
-        target = dot3(sent, square[...], NT)
-        target = jnp.where(iota((slots, width), 1) == levels_c, counts_out, target)
-        disp_send[:, :, 0:width] = target.reshape(n_col, cap, width)
         slot_left = jnp.concatenate([given[elements + 4 : elements + 5], given[elements + 5 : elements + 6]], axis=1)
         chosen_left = jnp.where(
             iota((slots, rows), 0) + (sec - 1) * slots == slot_left.astype(I32), 1.0, 0.0
@@ -271,8 +277,11 @@
         for k in range(4):
             near_left = near_left + jnp.where(nbr_left[k : k + 1, :] == here, 1.0, 0.0)
         reach_left = dot(dot(chosen_left, repeat, NT).astype(BF16), near_left.astype(BF16), NT)
-        extra = dot3(rate * pick(reach_left.astype(BF16), own), square[...], NT)
-        disp_send[:, :, width:] = extra.reshape(n_col, cap, width)
+        extra = rate * pick(reach_left.astype(BF16), own)
+        both = dot3(jnp.concatenate([sent, extra], axis=0), square[...], NT)
+        target = jnp.where(iota((slots, width), 1) == levels_c, counts_out, both[:slots])
+        disp_send[:, :, 0:width] = target.reshape(n_col, cap, width)
+        disp_send[:, :, width:] = both[slots:].reshape(n_col, cap, width)
 
         pl.semaphore_wait(barrier, n_col + 1)
         def send(other):
@@ -288,15 +297,19 @@
 
         fetches[7].wait()
         for f in range(2):
-            parts[f, levels_c:] = jnp.zeros((levels_h - levels_c, 8, slots), F32)
-
-            def widen(z, carry, f=f):
-                x = block[0, f, z].astype(F32)
+            parts[f, 8 * levels_c :] = jnp.zeros((8 * (levels_h - levels_c), slots), F32)
+
+        def widen(z, carry):
+            water = block[0, 1, z].astype(F32)
+            for f, x in ((1, water), (0, block[0, 0, z].astype(F32) + LATENT * water)):
                 plain[f][z] = x
-                parts[f, z] = (x[0:8] + x[8:16]) + (x[16:24] + x[24:32])
-                return carry
-
-            lax.fori_loop(0, levels_c, widen, 0, unroll=UNROLL)
+                parts[f, pl.ds(8 * z, 8), :] = (x[0:8] + x[8:16]) + (x[16:24] + x[24:32])
+            return carry
+
+        lax.fori_loop(0, levels_c, widen, 0, unroll=UNROLL)
+
+        def over_columns(f):
+            return sum(parts[f, pl.ds(k, levels_h, stride=8), :] for k in range(8))
 
         def strided(ref, z):
             return tuple(ref[z, pl.ds(k, 8, stride=4), :] for k in range(4))
@@ -334,7 +347,7 @@
             lax.fori_loop(0, levels_c, first, (edge, edge), unroll=UNROLL)
 
         columns_inv = 1.0 / across
-        start = [jnp.sum(parts[f], axis=1) * columns_inv for f in range(2)]
+        start = [over_columns(f) * columns_inv for f in range(2)]
         level = iota((levels_h, slots), 0)
         wet = jnp.concatenate([sat_ref[...], jnp.zeros((1, 128 - levels_c), F32)], axis=1)
         wet = jnp.transpose(jnp.broadcast_to(wet, (128, 128)))[:levels_h]
@@ -352,63 +365,57 @@
         counts = arrived[levels_c : levels_c + 1, :]
         counts8 = jnp.broadcast_to(counts, (8, slots))
         goal = [arrived[f * levels_h : (f + 1) * levels_h] for f in range(2)]
+        goal[0] = goal[0] + LATENT * goal[1]
         mean = list(start)
         offset = [jnp.zeros((levels_h, slots), F32)] * 2
 
         for n in range(MAX_SUB):
             scale = CENTRE ** (n + 1)
             keep = counts > float(n)
-            moved, shifted = [], []
-            for f in range(2):
-                d = RELAX * (goal[f] - mean[f])
-                moved.append(smoothed(mean[f] + d))
-                shifted.append(smoothed(offset[f] + d))
+            d = [RELAX * (goal[f] - mean[f]) for f in range(2)]
+            moved = smoothed(mean[0] + d[0])
+            shifted = [smoothed(offset[f] + d[f]) for f in range(2)]
             limit = (0.5 / scale) * (wet - shifted[1])
             limits[...] = limit if n == 0 else jnp.where(keep, limit, 0.0)
 
             def condense(water, z, by_half):
                 bound = jnp.broadcast_to(limits[pl.ds(z, 1), :], (8, slots))
-                drop = [jnp.maximum(by_half * water[k] - bound, 0.0) for k in range(4)]
-                parts[1, z] = (drop[0] + drop[1]) + (drop[2] + drop[3])
-                return [water[k] - drop[k] for k in range(4)], drop
+                new = [jnp.minimum(water[k], by_half * water[k] + bound) for k in range(4)]
+                parts[1, pl.ds(8 * z, 8), :] = (new[0] + new[1]) + (new[2] + new[3])
+                return new
 
             if n == 0:
 
                 def finish(z, carry):
-                    new, drop = condense(packed(water_a, z), z, 0.5)
-                    put_packed(water_b, z, new)
-                    put_packed(drops.at[0], z, drop)
+                    put_packed(water_b, z, condense(packed(water_a, z), z, 0.5))
                     return carry
 
                 lax.fori_loop(0, levels_c, finish, 0, unroll=UNROLL)
             else:
                 going = jnp.where(counts8 > float(n), 1.0, 0.0)
-                by_x, by_z, by_half = going * (HORIZ / CENTRE), going * (VERTIC / CENTRE), going * 0.5
+                by_x, by_z, by_half = going * (HORIZ / CENTRE), going * (VERTIC / CENTRE), 1.0 - going * 0.5
                 old, fresh = (water_b, water_a) if n % 2 else (water_a, water_b)
 
                 def sweep(z, carry, n=n, old=old, fresh=fresh, by_x=by_x, by_z=by_z, by_half=by_half):
                     below, here = carry
                     above = packed(old, jnp.minimum(z + 1, levels_c - 1))
-                    new, drop = condense(stencil(here, below, above, by_x, by_z), z, by_half)
+                    new = condense(stencil(here, below, above, by_x, by_z), z, by_half)
                     if n == MAX_SUB - 1:
                         put_strided(plain_water, z, new)
-                        put_strided(drops.at[n], z, drop)
                     else:
                         put_packed(fresh, z, new)
-                        put_packed(drops.at[n], z, drop)
                     return here, above
 
                 edge = packed(old, 0)
                 lax.fori_loop(0, levels_c, sweep, (edge, edge), unroll=UNROLL)
 
-            dried = jnp.sum(parts[1], axis=1) * (columns_inv * scale)
-            mean[0] = jnp.where(keep, moved[0] + LATENT * dried, mean[0])
-            mean[1] = jnp.where(keep, moved[1] - dried, mean[1])
+            dried = over_columns(1) * (columns_inv * scale) + shifted[1]
+            mean[0] = jnp.where(keep, moved, mean[0])
+            mean[1] = jnp.where(keep, dried, mean[1])
             offset = [jnp.where(keep, shifted[f], offset[f]) for f in range(2)]
 
-        change = jnp.concatenate(
-            [jnp.where(level < levels_c, mean[f] - start[f], 0.0) for f in range(2)], axis=0
-        )
+        gain = [jnp.where(level < levels_c, mean[f] - start[f], 0.0) for f in range(2)]
+        change = jnp.concatenate([gain[0] - LATENT * gain[1], gain[1]], axis=0)
         tendency = dot3(jnp.transpose(change), square[...])
         tend_send[...] = tendency.reshape(n_col, cap, width)
 
@@ -433,13 +440,9 @@
 
             old, fresh = (energy_a, energy_b) if n % 2 else (energy_b, energy_a)
 
-            def warmed(z, n=n, old=old):
-                energy, drop = packed(old, z), packed(drops.at[n - 1], z)
-                return tuple(energy[k] + LATENT * drop[k] for k in range(4))
-
-            def follow(z, carry, n=n, fresh=fresh, by_x=by_x, by_z=by_z, warmed=warmed):
+            def follow(z, carry, n=n, old=old, fresh=fresh, by_x=by_x, by_z=by_z):
                 below, here = carry
-                above = warmed(jnp.minimum(z + 1, levels_c - 1))
+                above = packed(old, jnp.minimum(z + 1, levels_c - 1))
                 new = stencil(here, below, above, by_x, by_z)
                 if n == MAX_SUB - 1:
                     put_strided(plain_energy, z, new)
@@ -447,7 +450,7 @@
                     put_packed(fresh, z, new)
                 return here, above
 
-            edge = warmed(0)
+            edge = packed(old, 0)
             lax.fori_loop(0, levels_c, follow, (edge, edge), unroll=UNROLL)
 
         power = jnp.full((1, slots), CENTRE, F32)
@@ -458,15 +461,17 @@
         for f in range(2):
             offsets[f] = offset[f]
 
-            def narrow(z, carry, f=f):
-                x = plain[f][z]
-                if f == 0:
-                    x = x + LATENT * drops[MAX_SUB - 1, z]
-                x = power * x + jnp.broadcast_to(offsets[f, pl.ds(z, 1), :], x.shape)
-                block[0, f, z] = jnp.where(used, x, block[0, f, z].astype(F32)).astype(BF16)
-                return carry
-
-            lax.fori_loop(0, levels_c, narrow, 0, unroll=UNROLL)
+        def narrow(z, carry):
+            x = [
+                power * plain[f][z] + jnp.broadcast_to(offsets[f, pl.ds(z, 1), :], power.shape)
+                for f in range(2)
+            ]
+            x[0] = x[0] - LATENT * x[1]
+            for f in range(2):
+                block[0, f, z] = jnp.where(used, x[f], block[0, f, z].astype(F32)).astype(BF16)
+            return carry
+
+        lax.fori_loop(0, levels_c, narrow, 0, unroll=UNROLL)
 
     @pl.when(jnp.logical_not(is_cloud))
     def _():
@@ -499,9 +504,9 @@
         )
 
     def gather(sources):
-        for source in sources:
-            found = tends[source].reshape(slots, width)
-            adv_ref[...] += pick(member[:, source * slots : (source + 1) * slots], found)
+        found = [tends[source].reshape(slots, width) for source in sources]
+        where = [member[:, source * slots : (source + 1) * slots] for source in sources]
+        adv_ref[...] += pick(jnp.concatenate(where, axis=1), jnp.concatenate(found, axis=0))
 
     for mine, theirs in (((1,), (0, 2)), ((0, 2), (1,))):
 
@@ -586,8 +591,7 @@
             pltpu.VMEM((levels_c, levels_h), F32),
             pltpu.VMEM((1, levels_c), F32),
             *[pltpu.VMEM((levels_c, across, slots), F32)] * 6,
-            pltpu.VMEM((MAX_SUB, levels_c, across, slots), F32),
-            pltpu.VMEM((fields, levels_h, 8, slots), F32),
+            pltpu.VMEM((fields, 8 * levels_h, slots), F32),
             pltpu.VMEM((levels_h, slots), F32),
             pltpu.VMEM((fields, levels_h, slots), F32),
             pltpu.VMEM((fields * levels_h, fields * levels_h), F32),

time: 35.4 us -> 35.2 us (level)
  no operation moved by 1% of the time
where the time goes in v4:
time: 35.2 us; the launch traced here: 35.1 us
  Pallas kernels  32.8 us (93%)
  local copies, waits for them, and re-layouts  1.59 us (5%)
  between operations  0.64 us (2%)
    pallas_call x1, Pallas kernels, body(): pl.pallas_call(functools.partial(kernel, (n_sec, n_col)), out_shape=tuple...  32.8 us
    unnamed x2, local copies, waits for them, and re-layouts  1.59 us

profile of v4, /device:TPU:1, one launch (start us, length us, event | category | flops | bytes accessed | tf_op | source)
XLA Modules:
  0.0 35.1 jit_solution(17743595689552298931)
XLA Ops:
  0.6 32.8 %shard_map.95 = (f32[256,128]{1,0:T(8,128)S(1)}, bf16[1,2,58,32,128]{4,3,2,1,0:T(8,128)(2,1)S(1)}) custom-call(f32[256,128]{1,0:T(8,128)} %cs_hbm.1, f32[1,128]{1,0:T(1,128)} %bitcast.8, s32[4,64]{1,0:T(4,128)} %bitcast.5, s32[1,256]{1,0:T(1,128)} %bitcast.6, s32[1,256]{1,0:T(1,128)} %bitcast.7, bf16[1,2,58,32,128]{4,3,2,1,0:T(8,128)(2,1)} %cloud_hbm.1, ...), custom_call_target="tpu_custom_call" | custom-call | tf_op jit(solution)/shard_map/pallas_call | solution.py:580
  33.5 0.7 %copy.12 = f32[256,128]{1,0:T(8,128)} copy(f32[256,128]{1,0:T(8,128)S(1)} %get-tuple-element.2) | data formatting | bytes 262144
  34.1 0.9 %copy.13 = bf16[1,2,58,32,128]{4,3,2,1,0:T(8,128)(2,1)} copy(bf16[1,2,58,32,128]{4,3,2,1,0:T(8,128)(2,1)S(1)} %get-tuple-element.3) | data formatting | bytes 1900544

commit v5 on v4

--- a/solution.py
+++ b/solution.py
@@ -169,9 +169,13 @@
 
     greet((sibling, col))
 
-    @pl.when(sec != 2)
+    @pl.when(core == 1)
     def _():
         greet((facing, col))
+
+    @pl.when(sec == 1)
+    def _():
+        greet((2, col))
 
     fetches[0].wait()
     fetches[1].wait()
@@ -226,6 +230,13 @@
         pl.semaphore_wait(barrier, n_sec + 1)
         for section in (2, 1):
             push(section).start()
+
+    def give(other, chip):
+        return pltpu.make_async_remote_copy(
+            src_ref=tend_send.at[other], dst_ref=tends.at[sec - 1, col],
+            send_sem=tend_send_sem.at[chip], recv_sem=tend_recv_sem.at[sec - 1],
+            device_id=(2 * chip + 1, other), device_id_type=MESH,
+        )
 
     for fetch in fetches[3:7]:
         fetch.wait()
@@ -419,20 +430,20 @@
         tendency = dot3(jnp.transpose(change), square[...])
         tend_send[...] = tendency.reshape(n_col, cap, width)
 
-        def give(other, chip):
-            pltpu.make_async_remote_copy(
-                src_ref=tend_send.at[other], dst_ref=tends.at[sec - 1, col],
-                send_sem=tend_send_sem.at[chip], recv_sem=tend_recv_sem.at[sec - 1],
-                device_id=((sec, facing)[chip], other), device_id_type=MESH,
-            ).start()
-
         def give_both(other):
-            give(other, 1)
-            give(other, 0)
+            for chip in range(2):
+                give(other, chip).start()
 
         for_others(col, give_both)
-        give(col, 1)
-        pltpu.make_async_copy(tend_send.at[col], tends.at[sec - 1, col], tend_recv_sem.at[sec - 1]).start()
+        for chip in range(2):
+
+            @pl.when(sec != 2 * chip + 1)
+            def _():
+                give(col, chip).start()
+
+        @pl.when(core == 1)
+        def _():
+            pltpu.make_async_copy(tend_send.at[col], tends.at[sec - 1, col], tend_recv_sem.at[sec - 1]).start()
 
         for n in range(1, MAX_SUB):
             going = jnp.where(counts8 > float(n), 1.0, 0.0)
@@ -503,24 +514,19 @@
             device_id=(sibling, col), device_id_type=MESH,
         )
 
-    def gather(sources):
-        found = [tends[source].reshape(slots, width) for source in sources]
-        where = [member[:, source * slots : (source + 1) * slots] for source in sources]
-        adv_ref[...] += pick(jnp.concatenate(where, axis=1), jnp.concatenate(found, axis=0))
-
-    for mine, theirs in (((1,), (0, 2)), ((0, 2), (1,))):
-
-        @pl.when(core == len(mine) - 1)
-        def _():
-            for source in mine:
-                heard(source)
-                passing(source).start()
-            gather(mine)
-            for source in theirs:
-                passing(source).wait_recv()
-            gather(theirs)
-
-    summed = adv_ref[...]
+    @pl.when(core == 1)
+    def _():
+        for source in range(n_sec - 1):
+            heard(source)
+            passing(source).start()
+
+    @pl.when(core == 0)
+    def _():
+        for source in range(n_sec - 1):
+            passing(source).wait_recv()
+
+    gathered = tends[...].reshape((n_sec - 1) * slots, width)
+    summed = adv_ref[...] + pick(member, gathered)
     out_ref[...] = jnp.where(
         iota((rows, width), 1) >= levels_h, jnp.maximum(summed, 0.0), summed
     )
@@ -536,19 +542,21 @@
 
     to_left.wait_send()
 
-    for mine in ((1,), (0, 2)):
-
-        @pl.when(core == len(mine) - 1)
-        def _():
-            for source in mine:
-                passing(source).wait_send()
+    @pl.when(core == 1)
+    def _():
+        for source in range(n_sec - 1):
+            passing(source).wait_send()
 
     @pl.when(is_cloud)
     def _():
         others = pl.ds(0, n_col - 1)
         pltpu.make_async_copy(disp_send.at[others], disp_send.at[others], disp_send_sem).wait()
-        pltpu.make_async_copy(tend_send.at[others], tend_send.at[others], tend_send_sem.at[0]).wait()
-        pltpu.make_async_copy(tend_send, tend_send, tend_send_sem.at[1]).wait()
+        for chip in range(2):
+            pltpu.make_async_copy(tend_send.at[others], tend_send.at[others], tend_send_sem.at[chip]).wait()
+
+            @pl.when(sec != 2 * chip + 1)
+            def _():
+                give(col, chip).wait_send()
 
 
 def body(

time: 35.2 us -> 34.5 us (0.980)
  Pallas kernels: 32.8 us -> 32.1 us
    pallas_call x1, Pallas kernels: 32.8 us -> 32.1 us  [body(): pl.pallas_call(functools.partial(kernel, (n_sec, n_col)), out_shape=tuple...]
where the time goes in v5:
time: 34.5 us; the launch traced here: 34.4 us
  Pallas kernels  32.1 us (93%)
  local copies, waits for them, and re-layouts  1.59 us (5%)
  between operations  0.64 us (2%)
    pallas_call x1, Pallas kernels, body(): pl.pallas_call(functools.partial(kernel, (n_sec, n_col)), out_shape=tuple...  32.1 us
    unnamed x2, local copies, waits for them, and re-layouts  1.59 us

profile of v5, /device:TPU:1, one launch (start us, length us, event | category | flops | bytes accessed | tf_op | source)
XLA Modules:
  0.0 34.4 jit_solution(1336446389964941145)
XLA Ops:
  0.6 32.1 %shard_map.95 = (f32[256,128]{1,0:T(8,128)S(1)}, bf16[1,2,58,32,128]{4,3,2,1,0:T(8,128)(2,1)S(1)}) custom-call(f32[256,128]{1,0:T(8,128)} %cs_hbm.1, f32[1,128]{1,0:T(1,128)} %bitcast.8, s32[4,64]{1,0:T(4,128)} %bitcast.5, s32[1,256]{1,0:T(1,128)} %bitcast.6, s32[1,256]{1,0:T(1,128)} %bitcast.7, bf16[1,2,58,32,128]{4,3,2,1,0:T(8,128)(2,1)} %cloud_hbm.1, ...), custom_call_target="tpu_custom_call" | custom-call | tf_op jit(solution)/shard_map/pallas_call | solution.py:588
  32.8 0.7 %copy.12 = f32[256,128]{1,0:T(8,128)} copy(f32[256,128]{1,0:T(8,128)S(1)} %get-tuple-element.2) | data formatting | bytes 262144
  33.4 0.9 %copy.13 = bf16[1,2,58,32,128]{4,3,2,1,0:T(8,128)(2,1)} copy(bf16[1,2,58,32,128]{4,3,2,1,0:T(8,128)(2,1)S(1)} %get-tuple-element.3) | data formatting | bytes 1900544

commit v6 on v5

--- a/solution.py
+++ b/solution.py
@@ -559,6 +559,17 @@
                 give(col, chip).wait_send()
 
 
+def write(columns, cloud, columns_out, cloud_out, sem):
+    copies = [
+        pltpu.make_async_copy(cloud, cloud_out, sem.at[0]),
+        pltpu.make_async_copy(columns, columns_out, sem.at[1]),
+    ]
+    for copy in copies:
+        copy.start()
+    for copy in copies:
+        copy.wait()
+
+
 def body(
     column_state, mixing_rate, neighbours, assignment, substeps, cloud_state, level_map, saturation
 ):
@@ -585,7 +596,7 @@
         level_map,
         saturation.reshape(1, levels_c),
     )
-    return pl.pallas_call(
+    columns, cloud = pl.pallas_call(
         functools.partial(kernel, (n_sec, n_col)),
         out_shape=tuple(pltpu.VMEM(r.shape, r.dtype) for r in results),
         in_specs=[hbm] * 8,
@@ -627,6 +638,15 @@
             collective_id=0, has_side_effects=True, vmem_limit_bytes=48 * 1024 * 1024
         ),
     )(*(pltpu.with_memory_space_constraint(x, pltpu.HBM) for x in operands))
+    anywhere = pl.BlockSpec(memory_space=pl.ANY)
+    return pl.pallas_call(
+        write,
+        out_shape=results,
+        in_specs=[anywhere, anywhere],
+        out_specs=(anywhere, anywhere),
+        scratch_shapes=[dma((2,))],
+        compiler_params=pltpu.CompilerParams(vmem_limit_bytes=1024 * 1024),
+    )(columns, cloud)
 
 
 def solution(mesh):

time: 34.5 us -> 33.9 us (0.983)
  local copies, waits for them, and re-layouts: 1.59 us -> 0 us
  Pallas kernels: 32.1 us -> 33.1 us
    unnamed x2 -> x0, local copies, waits for them, and re-layouts: 1.59 us -> none
    pallas_call x0 -> x1, Pallas kernels: none -> 0.99 us  [body(): pl.pallas_call(write, out_shape=results, in_specs=[anywhere, anywhere], o...]
where the time goes in v6:
time: 33.9 us; the launch traced here: 33.8 us
  Pallas kernels  33.1 us (98%)
  between operations  0.64 us (2%)
    pallas_call x1, Pallas kernels, body(): pl.pallas_call(functools.partial(kernel, (n_sec, n_col)), out_shape=tuple...  32.1 us
    pallas_call x1, Pallas kernels, body(): pl.pallas_call(write, out_shape=results, in_specs=[anywhere, anywhere], o...  0.99 us

profile of v6, /device:TPU:1, one launch (start us, length us, event | category | flops | bytes accessed | tf_op | source)
XLA Modules:
  0.0 33.8 jit_solution(16848362811875253046)
XLA Ops:
  0.6 32.1 %shard_map.95 = (f32[256,128]{1,0:T(8,128)S(1)}, bf16[1,2,58,32,128]{4,3,2,1,0:T(8,128)(2,1)S(1)}) custom-call(f32[256,128]{1,0:T(8,128)} %cs_hbm.1, f32[1,128]{1,0:T(1,128)} %bitcast.8, s32[4,64]{1,0:T(4,128)} %bitcast.5, s32[1,256]{1,0:T(1,128)} %bitcast.6, s32[1,256]{1,0:T(1,128)} %bitcast.7, bf16[1,2,58,32,128]{4,3,2,1,0:T(8,128)(2,1)} %cloud_hbm.1, ...), custom_call_target="tpu_custom_call" | custom-call | tf_op jit(solution)/shard_map/pallas_call | solution.py:599
  32.8 1.0 %shard_map.96 = (f32[256,128]{1,0:T(8,128)}, bf16[1,2,58,32,128]{4,3,2,1,0:T(8,128)(2,1)}) custom-call(f32[256,128]{1,0:T(8,128)S(1)} %get-tuple-element.4.columns, bf16[1,2,58,32,128]{4,3,2,1,0:T(8,128)(2,1)S(1)} %get-tuple-element.5.cloud), custom_call_target="tpu_custom_call" | custom-call | tf_op jit(solution)/shard_map/pallas_call | solution.py:642

commit v7 on v6

--- a/solution.py
+++ b/solution.py
@@ -430,12 +430,8 @@
         tendency = dot3(jnp.transpose(change), square[...])
         tend_send[...] = tendency.reshape(n_col, cap, width)
 
-        def give_both(other):
-            for chip in range(2):
-                give(other, chip).start()
-
-        for_others(col, give_both)
         for chip in range(2):
+            for_others(col, lambda other, chip=chip: give(other, chip).start())
 
             @pl.when(sec != 2 * chip + 1)
             def _():
@@ -519,14 +515,16 @@
         for source in range(n_sec - 1):
             heard(source)
             passing(source).start()
+        adv_ref[...] += pick(member, tends[...].reshape((n_sec - 1) * slots, width))
 
     @pl.when(core == 0)
     def _():
         for source in range(n_sec - 1):
             passing(source).wait_recv()
-
-    gathered = tends[...].reshape((n_sec - 1) * slots, width)
-    summed = adv_ref[...] + pick(member, gathered)
+            found = tends[source].reshape(slots, width)
+            adv_ref[...] += pick(member[:, source * slots : (source + 1) * slots], found)
+
+    summed = adv_ref[...]
     out_ref[...] = jnp.where(
         iota((rows, width), 1) >= levels_h, jnp.maximum(summed, 0.0), summed
     )

time: 33.9 us -> 33 us (0.973)
  Pallas kernels: 33.1 us -> 32.3 us
    pallas_call x1, Pallas kernels: 32.1 us -> 31.3 us  [body(): pl.pallas_call(functools.partial(kernel, (n_sec, n_col)), out_shape=tuple...]
where the time goes in v7:
time: 33 us; the launch traced here: 32.9 us
  Pallas kernels  32.3 us (98%)
  between operations  0.64 us (2%)
    pallas_call x1, Pallas kernels, body(): pl.pallas_call(functools.partial(kernel, (n_sec, n_col)), out_shape=tuple...  31.3 us
    pallas_call x1, Pallas kernels, body(): pl.pallas_call(write, out_shape=results, in_specs=[anywhere, anywhere], o...  0.99 us

profile of v7, /device:TPU:1, one launch (start us, length us, event | category | flops | bytes accessed | tf_op | source)
XLA Modules:
  0.0 32.9 jit_solution(9916178884061512865)
XLA Ops:
  0.6 31.3 %shard_map.95 = (f32[256,128]{1,0:T(8,128)S(1)}, bf16[1,2,58,32,128]{4,3,2,1,0:T(8,128)(2,1)S(1)}) custom-call(f32[256,128]{1,0:T(8,128)} %cs_hbm.1, f32[1,128]{1,0:T(1,128)} %bitcast.8, s32[4,64]{1,0:T(4,128)} %bitcast.5, s32[1,256]{1,0:T(1,128)} %bitcast.6, s32[1,256]{1,0:T(1,128)} %bitcast.7, bf16[1,2,58,32,128]{4,3,2,1,0:T(8,128)(2,1)} %cloud_hbm.1, ...), custom_call_target="tpu_custom_call" | custom-call | tf_op jit(solution)/shard_map/pallas_call | solution.py:597
  32.0 1.0 %shard_map.96 = (f32[256,128]{1,0:T(8,128)}, bf16[1,2,58,32,128]{4,3,2,1,0:T(8,128)(2,1)}) custom-call(f32[256,128]{1,0:T(8,128)S(1)} %get-tuple-element.4.columns, bf16[1,2,58,32,128]{4,3,2,1,0:T(8,128)(2,1)S(1)} %get-tuple-element.5.cloud), custom_call_target="tpu_custom_call" | custom-call | tf_op jit(solution)/shard_map/pallas_call | solution.py:640

commit v8 on v7

--- a/solution.py
+++ b/solution.py
@@ -275,6 +275,7 @@
         reach = dot(by_element, near_t, NT).astype(BF16)
         known = pick(chosen16, base) + rate * pick(reach[:, 2 * elements :], own)
         reach = reach[:, :elements]
+        mapped = dot3(rate * own, square[...], NT)
 
         push_arrives()
         sent = known + rate * pick(reach, given[0:elements])
@@ -288,11 +289,11 @@
         for k in range(4):
             near_left = near_left + jnp.where(nbr_left[k : k + 1, :] == here, 1.0, 0.0)
         reach_left = dot(dot(chosen_left, repeat, NT).astype(BF16), near_left.astype(BF16), NT)
-        extra = rate * pick(reach_left.astype(BF16), own)
-        both = dot3(jnp.concatenate([sent, extra], axis=0), square[...], NT)
-        target = jnp.where(iota((slots, width), 1) == levels_c, counts_out, both[:slots])
+        extra = pick(reach_left.astype(BF16), mapped)
+        target = dot3(sent, square[...], NT)
+        target = jnp.where(iota((slots, width), 1) == levels_c, counts_out, target)
         disp_send[:, :, 0:width] = target.reshape(n_col, cap, width)
-        disp_send[:, :, width:] = both[slots:].reshape(n_col, cap, width)
+        disp_send[:, :, width:] = extra.reshape(n_col, cap, width)
 
         pl.semaphore_wait(barrier, n_col + 1)
         def send(other):
@@ -367,6 +368,10 @@
             up = jnp.where(level == levels_c - 1, x, pltpu.roll(x, levels_h - 1, axis=0))
             low = jnp.where(level == 0, x, pltpu.roll(x, 1, axis=0))
             return (1.0 - 2.0 * VERTIC) * x + VERTIC * (up + low)
+
+        untouched = [start[0]]
+        for _ in range(MAX_SUB):
+            untouched.append(smoothed(untouched[-1]))
 
         pltpu.make_async_copy(disp_recv, disp_recv, disp_recv_sem).wait()
         later = disp_recv[:, :, width:].reshape(slots, width)
@@ -384,7 +389,6 @@
             scale = CENTRE ** (n + 1)
             keep = counts > float(n)
             d = [RELAX * (goal[f] - mean[f]) for f in range(2)]
-            moved = smoothed(mean[0] + d[0])
             shifted = [smoothed(offset[f] + d[f]) for f in range(2)]
             limit = (0.5 / scale) * (wet - shifted[1])
             limits[...] = limit if n == 0 else jnp.where(keep, limit, 0.0)
@@ -421,7 +425,7 @@
                 lax.fori_loop(0, levels_c, sweep, (edge, edge), unroll=UNROLL)
 
             dried = over_columns(1) * (columns_inv * scale) + shifted[1]
-            mean[0] = jnp.where(keep, moved, mean[0])
+            mean[0] = jnp.where(keep, untouched[n + 1] + shifted[0], mean[0])
             mean[1] = jnp.where(keep, dried, mean[1])
             offset = [jnp.where(keep, shifted[f], offset[f]) for f in range(2)]
 

time: 33 us -> 32.9 us (level)
  no operation moved by 1% of the time
where the time goes in v8:
time: 32.9 us; the launch traced here: 32.8 us
  Pallas kernels  32.2 us (98%)
  between operations  0.64 us (2%)
    pallas_call x1, Pallas kernels, body(): pl.pallas_call(functools.partial(kernel, (n_sec, n_col)), out_shape=tuple...  31.2 us
    pallas_call x1, Pallas kernels, body(): pl.pallas_call(write, out_shape=results, in_specs=[anywhere, anywhere], o...  0.99 us

profile of v8, /device:TPU:1, one launch (start us, length us, event | category | flops | bytes accessed | tf_op | source)
XLA Modules:
  0.0 32.8 jit_solution(3269329608635620050)
XLA Ops:
  0.6 31.2 %shard_map.95 = (f32[256,128]{1,0:T(8,128)S(1)}, bf16[1,2,58,32,128]{4,3,2,1,0:T(8,128)(2,1)S(1)}) custom-call(f32[256,128]{1,0:T(8,128)} %cs_hbm.1, f32[1,128]{1,0:T(1,128)} %bitcast.8, s32[4,64]{1,0:T(4,128)} %bitcast.5, s32[1,256]{1,0:T(1,128)} %bitcast.6, s32[1,256]{1,0:T(1,128)} %bitcast.7, bf16[1,2,58,32,128]{4,3,2,1,0:T(8,128)(2,1)} %cloud_hbm.1, ...), custom_call_target="tpu_custom_call" | custom-call | tf_op jit(solution)/shard_map/pallas_call | solution.py:601
  31.8 1.0 %shard_map.96 = (f32[256,128]{1,0:T(8,128)}, bf16[1,2,58,32,128]{4,3,2,1,0:T(8,128)(2,1)}) custom-call(f32[256,128]{1,0:T(8,128)S(1)} %get-tuple-element.4.columns, bf16[1,2,58,32,128]{4,3,2,1,0:T(8,128)(2,1)S(1)} %get-tuple-element.5.cloud), custom_call_target="tpu_custom_call" | custom-call | tf_op jit(solution)/shard_map/pallas_call | solution.py:644

commit v9 on v8

--- a/solution.py
+++ b/solution.py
@@ -206,7 +206,7 @@
             device_id=(section, right), device_id_type=MESH,
         )
 
-    relays = (sec == 1) | (sec == 2)
+    relays = sec == 1
     relay = pltpu.make_async_remote_copy(
         src_ref=given, dst_ref=given, send_sem=relay_sem, recv_sem=push_recv_sem,
         device_id=(sibling, col), device_id_type=MESH,
@@ -228,7 +228,7 @@
     @pl.when(jnp.logical_not(is_cloud))
     def _():
         pl.semaphore_wait(barrier, n_sec + 1)
-        for section in (2, 1):
+        for section in (2, 1, 3):
             push(section).start()
 
     def give(other, chip):
@@ -535,7 +535,7 @@
 
     @pl.when(jnp.logical_not(is_cloud))
     def _():
-        for section in (2, 1):
+        for section in (2, 1, 3):
             push(section).wait_send()
 
     @pl.when(relays)
@@ -625,7 +625,7 @@
             pltpu.VMEM((n_sec - 1,) + message, F32),
             pltpu.VMEM((rows, width), F32),
             dma((8,)),
-            dma((2,)),
+            dma((3,)),
             dma,
             dma,
             dma((2,)),

time: 32.9 us -> 33.1 us (level)
  no operation moved by 1% of the time
where the time goes in v9:
time: 33.1 us; the launch traced here: 33 us
  Pallas kernels  32.3 us (98%)
  between operations  0.64 us (2%)
    pallas_call x1, Pallas kernels, body(): pl.pallas_call(functools.partial(kernel, (n_sec, n_col)), out_shape=tuple...  31.3 us
    pallas_call x1, Pallas kernels, body(): pl.pallas_call(write, out_shape=results, in_specs=[anywhere, anywhere], o...  0.99 us

profile of v9, /device:TPU:1, one launch (start us, length us, event | category | flops | bytes accessed | tf_op | source)
XLA Modules:
  0.0 33.0 jit_solution(7579886428886665286)
XLA Ops:
  0.6 31.3 %shard_map.95 = (f32[256,128]{1,0:T(8,128)S(1)}, bf16[1,2,58,32,128]{4,3,2,1,0:T(8,128)(2,1)S(1)}) custom-call(f32[256,128]{1,0:T(8,128)} %cs_hbm.1, f32[1,128]{1,0:T(1,128)} %bitcast.8, s32[4,64]{1,0:T(4,128)} %bitcast.5, s32[1,256]{1,0:T(1,128)} %bitcast.6, s32[1,256]{1,0:T(1,128)} %bitcast.7, bf16[1,2,58,32,128]{4,3,2,1,0:T(8,128)(2,1)} %cloud_hbm.1, ...), custom_call_target="tpu_custom_call" | custom-call | tf_op jit(solution)/shard_map/pallas_call | solution.py:601
  32.0 1.0 %shard_map.96 = (f32[256,128]{1,0:T(8,128)}, bf16[1,2,58,32,128]{4,3,2,1,0:T(8,128)(2,1)}) custom-call(f32[256,128]{1,0:T(8,128)S(1)} %get-tuple-element.4.columns, bf16[1,2,58,32,128]{4,3,2,1,0:T(8,128)(2,1)S(1)} %get-tuple-element.5.cloud), custom_call_target="tpu_custom_call" | custom-call | tf_op jit(solution)/shard_map/pallas_call | solution.py:644
